TPU v7x, 512 devices: a whole 4x4x16 slice. The times are simulated.
512 devices in a mesh: section: 8 (over y, core), dp: 64 (over z, x).
Axes of the slice: x: 4, y: 4, z: 16, core: 2. Of those that a mesh axis runs over, the one named last changes fastest.
Arguments:
- inputs: bfloat16 [16, 1024, 4096], P(None, 'dp'), may hold values from -6 to 6
- stashed: bfloat16 [8, 4096, 256], P('section', 'dp')
- master: float32 [8, 4096, 256], P('section', 'dp')
- first_moment: float32 [8, 4096, 256], P('section', 'dp'), may hold values from -0.0018 to 0.0018
- second_moment: float32 [8, 4096, 256], P('section', 'dp'), may hold values from 1e-08 to 1e-06
- counts: int32 [64, 16], P('dp'), may hold values from 1 to 16
- plan: int32 [16], replicated, may hold values from 0 to 15, each once
- layer_index: int32 [8], P('section'), may hold values from 0 to 47
Outputs:
- probe_out: bfloat16 [8, 1024, 4096], P('section', 'dp')
- new_master: float32 [8, 4096, 256], P('section', 'dp')
- new_first: float32 [8, 4096, 256], P('section', 'dp')
- new_second: float32 [8, 4096, 256], P('section', 'dp')
All inputs are finite; a program needn't handle non-finite values.
Results may differ from a plain program's by a relative error of at most 0.0095.
Values may be sent and summed in bfloat16 or wider, within the bound.
A program may use at most 64 MiB of HBM per device.

v0:
```python
import jax
import jax.numpy as jnp
from jax import lax
from jax.sharding import PartitionSpec as P

eps_norm = 1e-05
beta_one = 0.9
beta_two = 0.95
eps_adam = 1e-08
learn_rate = 0.002
decay_rate = 0.1


def shifted(x, axis, by):
    devices = lax.axis_size(axis)
    pairs = [(i, i + by) for i in range(devices) if 0 <= i + by < devices]
    return lax.ppermute(x, axis, pairs)


def branch_scale(layer_index):
    return lax.rsqrt(1.0 + layer_index.astype(jnp.float32) / 8.0)


def normalize(inputs):
    values = inputs.astype(jnp.float32)
    centred = values - jnp.mean(values, axis=-1, keepdims=True)
    inv_spread = lax.rsqrt(jnp.mean(centred * centred, axis=-1, keepdims=True) + eps_norm)
    return (values, centred * inv_spread, inv_spread)


def contract_last(lhs_array, rhs_array):
    return lax.dot_general(
        lhs_array, rhs_array, (((1,), (1,)), ((), ())), preferred_element_type=jnp.float32
    )


def contract_first(lhs_array, rhs_array):
    return lax.dot_general(
        lhs_array, rhs_array, (((0,), (0,)), ((), ())), preferred_element_type=jnp.float32
    )


def layer_forward(inputs, weight, gain_value, hid_width):
    values, normed, _ = normalize(inputs)
    normed_b = normed.astype(jnp.bfloat16)
    pre_act = jnp.dot(normed_b, weight[:, :hid_width], preferred_element_type=jnp.float32)
    hidden_b = jax.nn.gelu(pre_act).astype(jnp.bfloat16)
    branch_out = contract_last(hidden_b, weight[:, hid_width:])
    return (values + gain_value * branch_out).astype(jnp.bfloat16)


def layer_backward(inputs, grad_out, weight, gain_value, hid_width):
    values, normed, inv_spread = normalize(inputs)
    normed_b = normed.astype(jnp.bfloat16)
    w_in = weight[:, :hid_width]
    w_out = weight[:, hid_width:]
    pre_act = jnp.dot(normed_b, w_in, preferred_element_type=jnp.float32)
    gelu_value, gelu_back = jax.vjp(jax.nn.gelu, pre_act)
    hidden_b = gelu_value.astype(jnp.bfloat16)
    grad_float = grad_out.astype(jnp.float32)
    out_b = (gain_value * grad_float).astype(jnp.bfloat16)
    hidden_grad = jnp.dot(out_b, w_out, preferred_element_type=jnp.float32)
    pre_b = gelu_back(hidden_grad)[0].astype(jnp.bfloat16)
    normed_grad = contract_last(pre_b, w_in)
    grad_mean = jnp.mean(normed_grad, axis=-1, keepdims=True)
    cross_mean = jnp.mean(normed_grad * normed, axis=-1, keepdims=True)
    grad_in = (grad_float + inv_spread * (normed_grad - grad_mean - normed * cross_mean)).astype(
        jnp.bfloat16
    )
    return (grad_in, normed_b, pre_b, out_b, hidden_b)


def fetch_rows(shard_rows):
    return lax.all_gather(shard_rows, "dp", axis=0, tiled=True)


def pass_along(block_data, offset):
    return shifted(block_data, "section", offset)


def shards(inputs, stashed, master, first_moment, second_moment, counts, plan, layer_index):
    sections = lax.axis_size("section")
    position = lax.axis_index("section")
    micro_count = inputs.shape[0]
    tok_rows = inputs.shape[1]
    model_width = inputs.shape[2]
    hid_width = master.shape[2] // 2
    gain_value = branch_scale(layer_index)[0]
    group_size = 1
    groups_all = micro_count // group_size
    block_rows = group_size * tok_rows
    tick_count = groups_all + sections - 1
    old_weight = fetch_rows(stashed[0])
    row_pos = lax.broadcasted_iota(jnp.int32, (group_size, tok_rows), 1)
    zero_model = jnp.zeros((block_rows, model_width), jnp.bfloat16)
    zero_hidden = jnp.zeros((block_rows, hid_width), jnp.bfloat16)
    buffer_model = jnp.zeros((groups_all + 1, block_rows, model_width), jnp.bfloat16)
    buffer_hidden = jnp.zeros((groups_all + 1, block_rows, hid_width), jnp.bfloat16)

    def members_of(slot_group):
        return lax.dynamic_slice_in_dim(plan, slot_group * group_size, group_size)

    def slot_info(tick_idx, lag_steps):
        slot_group = tick_idx - lag_steps
        active = (slot_group >= 0) & (slot_group < groups_all)
        safe_group = jnp.clip(slot_group, 0, groups_all - 1)
        write_at = jnp.where(active, slot_group, groups_all)
        return (active, safe_group, write_at)

    def run_forward(entering):
        return layer_forward(entering, old_weight, gain_value, hid_width)

    def skip_forward(entering):
        return jnp.zeros_like(entering)

    def forward_tick(tick_idx, loop_state):
        arriving, kept_inputs, start_grads = loop_state
        active, safe_group, write_at = slot_info(tick_idx, position)
        members = members_of(safe_group)
        fed_rows = jnp.take(inputs, members, axis=0).reshape(block_rows, model_width)
        entering = jnp.where(position == 0, fed_rows, arriving)
        leaving = lax.cond(active, run_forward, skip_forward, entering)
        limits = jnp.take(counts[0], members)
        valid_rows = (row_pos < limits[:, None]).reshape(block_rows, 1)
        masked = jnp.where(valid_rows, leaving, jnp.zeros_like(leaving))
        kept_inputs = lax.dynamic_update_index_in_dim(kept_inputs, entering, write_at, 0)
        start_grads = lax.dynamic_update_index_in_dim(start_grads, masked, write_at, 0)
        return (pass_along(leaving, 1), kept_inputs, start_grads)

    _, kept_inputs, start_grads = lax.fori_loop(
        0, tick_count, forward_tick, (zero_model, buffer_model, buffer_model)
    )

    def run_backward(saved_in, incoming):
        return layer_backward(saved_in, incoming, old_weight, gain_value, hid_width)

    def skip_backward(saved_in, incoming):
        return (zero_model, zero_model, zero_hidden, zero_model, zero_hidden)

    def backward_tick(tick_idx, loop_state):
        arriving, normed_buf, pre_buf, out_buf, hidden_buf = loop_state
        active, safe_group, write_at = slot_info(tick_idx, sections - 1 - position)
        saved_in = kept_inputs[safe_group]
        incoming = jnp.where(position == sections - 1, start_grads[safe_group], arriving)
        grad_in, normed_b, pre_b, out_b, hidden_b = lax.cond(
            active, run_backward, skip_backward, saved_in, incoming
        )
        normed_buf = lax.dynamic_update_index_in_dim(normed_buf, normed_b, write_at, 0)
        pre_buf = lax.dynamic_update_index_in_dim(pre_buf, pre_b, write_at, 0)
        out_buf = lax.dynamic_update_index_in_dim(out_buf, out_b, write_at, 0)
        hidden_buf = lax.dynamic_update_index_in_dim(hidden_buf, hidden_b, write_at, 0)
        return (pass_along(grad_in, -1), normed_buf, pre_buf, out_buf, hidden_buf)

    _, normed_buf, pre_buf, out_buf, hidden_buf = lax.fori_loop(
        0,
        tick_count,
        backward_tick,
        (zero_model, buffer_model, buffer_hidden, buffer_model, buffer_hidden),
    )
    total_rows = groups_all * block_rows
    normed_all = normed_buf[:groups_all].reshape(total_rows, model_width)
    pre_all = pre_buf[:groups_all].reshape(total_rows, hid_width)
    out_all = out_buf[:groups_all].reshape(total_rows, model_width)
    hidden_all = hidden_buf[:groups_all].reshape(total_rows, hid_width)
    grad_share = lax.psum_scatter(
        jnp.concatenate(
            [contract_first(normed_all, pre_all), contract_first(out_all, hidden_all)], axis=1
        ),
        "dp",
        scatter_dimension=0,
        tiled=True,
    )
    norm_sq = lax.psum(jnp.sum(grad_share * grad_share), ("section", "dp"))
    clip_factor = 1.0 / jnp.maximum(jnp.sqrt(norm_sq), 1.0)
    clipped = grad_share * clip_factor
    master_now = master[0]
    new_first = beta_one * first_moment[0] + (1.0 - beta_one) * clipped
    new_second = beta_two * second_moment[0] + (1.0 - beta_two) * clipped * clipped
    new_master = master_now - learn_rate * (
        new_first / (jnp.sqrt(new_second) + eps_adam) + decay_rate * master_now
    )
    fresh_weight = fetch_rows(new_master.astype(jnp.bfloat16))
    probe_in = kept_inputs[groups_all - 1, (group_size - 1) * tok_rows :, :]
    probe_out = layer_forward(probe_in, fresh_weight, gain_value, hid_width)
    return (probe_out[None], new_master[None], new_first[None], new_second[None])


def solution(mesh):
    in_specs = (
        P(None, "dp", None),
        P("section", "dp", None),
        P("section", "dp", None),
        P("section", "dp", None),
        P("section", "dp", None),
        P("dp", None),
        P(),
        P("section"),
    )
    out_specs = (
        P("section", "dp", None),
        P("section", "dp", None),
        P("section", "dp", None),
        P("section", "dp", None),
    )
    return jax.shard_map(shards, mesh=mesh, in_specs=in_specs, out_specs=out_specs, check_vma=False)
```

profile of v0, /device:TPU:24, one launch (start us, length us, event | category | flops | bytes accessed | tf_op | source)
XLA Modules:
  0.0 1733.1 jit_solution(15596960083727490347)
XLA Ops:
  8.6 147.5 %all-gather.6.cloned.1.call-done = bf16[1,4096,256]{2,1,0:T(8,128)(2,1)} async-done(((bf16[1,64,256]{2,1,0:T(8,128)(2,1)}), bf16[1,4096,256]{2,1,0:T(8,128)(2,1)}) %all-gather.6.cloned.1.call-update) | async-done | bytes 2097168 | tf_op jit(solution)/shard_map/all_gather | solution.py:74
  158.1 272.6 %while.45 = (s32[]{:T(128)}, bf16[16,4096]{1,0:T(8,128)(2,1)S(1)}, bf16[17,16,4096]{2,1,0:T(8,128)(2,1)S(1)}, bf16[17,16,4096]{2,1,0:T(8,128)(2,1)}, s32[]{:T(12...) while((s32[]{:T(128)}, bf16[16,4096]{1,0:T(8,128)(2,1)S(1)}, ...), condition=%wide.region_5.6_spmd.clone, body=%wide.region_0.5_spmd.clone.sunk | while | flops 34687024 | bytes 4065192 | solution.py:130
  215.6 4.0 collective-permute-done.1
  223.3 2.6 conditional.6
  235.9 2.6 conditional.6
  248.4 2.6 conditional.6
  261.0 2.6 conditional.6
  273.6 2.6 conditional.6
  286.1 2.6 conditional.6
  298.7 2.6 conditional.6
  311.3 2.6 conditional.6
  323.8 2.6 conditional.6
  336.4 2.6 conditional.6
  349.0 2.6 conditional.6
  361.5 2.6 conditional.6
  374.1 2.6 conditional.6
  386.7 2.6 conditional.6
  399.2 2.6 conditional.6
  411.8 2.6 conditional.6
  434.0 322.5 %while.44 = (s32[]{:T(128)}, bf16[16,4096]{1,0:T(8,128)(2,1)S(1)}, bf16[17,16,4096]{2,1,0:T(8,128)(2,1)S(1)}, bf16[17,16,128]{2,1,0:T(8,128)(2,1)S(1)}, bf16[17,...) while((s32[]{:T(128)}, bf16[16,4096]{1,0:T(8,128)(2,1)S(1)}, ...), condition=%wide.region_15.16_spmd, body=%wide.region_8.15_spmd.sunk | while | flops 52815896 | bytes 14998795 | solution.py:154
  438.0 4.8 collective-permute-done
  442.8 9.6 conditional.5
  456.9 9.6 conditional.5
  466.6 3.8 collective-permute-start
  472.8 9.6 conditional.5
  482.5 3.8 collective-permute-start
  488.8 9.6 conditional.5
  498.4 3.8 collective-permute-start
  504.7 9.6 conditional.5
  514.4 3.8 collective-permute-start
  520.6 9.6 conditional.5
  530.3 3.8 collective-permute-start
  536.6 9.6 conditional.5
  546.2 3.8 collective-permute-start
  552.5 9.6 conditional.5
  562.1 3.8 collective-permute-start
  568.4 9.6 conditional.5
  578.1 3.8 collective-permute-start
  584.4 9.6 conditional.5
  594.0 3.8 collective-permute-start
  600.3 9.6 conditional.5
  609.9 3.8 collective-permute-start
  616.2 9.6 conditional.5
  625.9 3.8 collective-permute-start
  632.2 9.6 conditional.5
  641.8 3.8 collective-permute-start
  648.1 9.6 conditional.5
  657.7 3.8 collective-permute-start
  664.0 9.6 conditional.5
  673.7 3.8 collective-permute-start
  680.0 9.6 conditional.5
  689.6 3.8 collective-permute-start
  696.5 12.8 collective-permute-start
  712.5 3.8 collective-permute-start
  719.4 6.7 collective-permute-start
  729.3 3.8 collective-permute-start
  736.2 10.9 collective-permute-start
  750.3 3.8 collective-permute-start
  758.7 2.4 pad_maximum_fusion
  761.1 5.6 copy.25
  767.8 715.4 %reduce-scatter.4.cloned.1.call-done = f32[64,256]{1,0:T(8,128)} async-done(((f32[4096,256]{1,0:T(8,128)}), f32[64,256]{1,0:T(8,128)}) %reduce-scatter.4.cloned.1.call-update) | async-done | bytes 65552
  1484.8 99.8 %psum.7 = f32[]{:T(128)} all-reduce(f32[]{:T(128)} %multiply_reduce_fusion), channel_id=1, replica_groups=mesh['section'=8,'dp'=64] {'section','dp'}, use_global_device_ids=true, to_apply=%region_18.19 | all-reduce | flops 1 | bytes 8 | tf_op jit(solution)/shard_map/psum | solution.py:173
  1590.5 133.1 %all-gather.4.cloned.1.call-done = bf16[4096,256]{1,0:T(8,128)(2,1)} async-done(((bf16[64,256]{1,0:T(8,128)(2,1)}), bf16[4096,256]{1,0:T(8,128)(2,1)}) %all-gather.4.cloned.1.call-update) | async-done | bytes 2097168 | tf_op jit(solution)/shard_map/all_gather | solution.py:74
  1723.6 2.9 fusion.83
  (634 shorter events, 459.3 us)
Async XLA Ops:
  7.2 149.0 %all-gather.6.cloned.1.call-start = ((), (), s32[]{:S(2)}) async-start(), calls=%async_computation.2 | async-start | bytes 2129920 | tf_op jit(solution)/shard_map/all_gather | solution.py:74
  7.9 1475.2 %reduce-scatter.4.cloned.1.call-start = ((), (), s32[]{:S(2)}) async-start(), calls=%async_computation.3 | async-start | bytes 4259840
  161.8 6.3 collective-permute-start.1
  171.8 6.3 collective-permute-start.1
  181.8 6.3 collective-permute-start.1
  191.7 6.3 collective-permute-start.1
  201.7 6.3 collective-permute-start.1
  211.7 8.0 collective-permute-start.1
  225.9 6.3 collective-permute-start.1
  238.5 6.3 collective-permute-start.1
  251.0 6.3 collective-permute-start.1
  263.6 6.3 collective-permute-start.1
  276.2 6.3 collective-permute-start.1
  288.8 6.3 collective-permute-start.1
  301.3 6.3 collective-permute-start.1
  313.9 6.3 collective-permute-start.1
  326.5 6.3 collective-permute-start.1
  339.0 6.3 collective-permute-start.1
  351.6 6.3 collective-permute-start.1
  364.2 6.3 collective-permute-start.1
  376.7 6.3 collective-permute-start.1
  389.3 6.3 collective-permute-start.1
  401.9 6.3 collective-permute-start.1
  414.4 6.3 collective-permute-start.1
  424.4 6.3 collective-permute-start.1
  434.7 8.1 collective-permute-start
  442.8 6.1 copy-start.2
  452.5 4.4 collective-permute-start
  456.9 6.1 copy-start.2
  466.6 6.3 collective-permute-start
  472.8 6.1 copy-start.2
  482.5 6.3 collective-permute-start
  488.8 6.1 copy-start.2
  498.4 6.3 collective-permute-start
  504.7 6.1 copy-start.2
  514.4 6.3 collective-permute-start
  520.6 6.1 copy-start.2
  530.3 6.3 collective-permute-start
  536.6 6.1 copy-start.2
  546.2 6.3 collective-permute-start
  552.5 6.1 copy-start.2
  562.1 6.3 collective-permute-start
  568.4 6.1 copy-start.2
  578.1 6.3 collective-permute-start
  584.4 6.1 copy-start.2
  594.0 6.3 collective-permute-start
  600.3 6.1 copy-start.2
  609.9 6.3 collective-permute-start
  616.2 6.1 copy-start.2
  625.9 6.3 collective-permute-start
  632.2 6.1 copy-start.2
  641.8 6.3 collective-permute-start
  648.1 6.1 copy-start.2
  657.7 6.3 collective-permute-start
  673.7 6.3 collective-permute-start
  689.6 6.3 collective-permute-start
  696.5 15.3 collective-permute-start
  712.5 6.3 collective-permute-start
  719.4 9.2 collective-permute-start
  729.3 6.3 collective-permute-start
  736.2 13.4 collective-permute-start
  750.3 6.3 collective-permute-start
  766.7 718.0 %copy-start.5 = (f32[1,64,256]{2,1,0:T(8,128)S(1)}, f32[1,64,256]{2,1,0:T(8,128)}, u32[]{:S(2)}) copy-start(f32[1,64,256]{2,1,0:T(8,128)} %param.20) | copy-start | bytes 196612
  766.8 956.9 %all-gather.4.cloned.1.call-start = ((), (), s32[]{:S(2)}) async-start(), calls=%async_computation.1 | async-start | bytes 2129920 | tf_op jit(solution)/shard_map/all_gather | solution.py:74
  (8 other events, 20.9 us)
Sparse Core Ops, SparseCore 0:
  10.9 145.1 all-gather.5
  766.9 716.1 reduce-scatter.3
  1586.3 137.2 all-gather.3
where the time goes:
time: 1740 us; the launch traced here: 1730 us
  waiting for transfers between devices  1080 us (62%)
  other arithmetic  151 us (9%)
  starting transfers between devices  147 us (8%)
  matrix products  121 us (7%)
  blocking collectives  99.8 us (6%)
  local copies, waits for them, and re-layouts  67.5 us (4%)
  loops' own time  49.3 us (3%)
    unnamed x4, waiting for transfers between devices  716 us
    all_gather x2, waiting for transfers between devices, fetch_rows(): return lax.all_gather(shard_rows, 'dp', axis=0, tiled=True)  281 us
    ppermute x46, starting transfers between devices, shifted(): return lax.ppermute(x, axis, pairs)  146 us
    psum x1, blocking collectives, shards(): norm_sq = lax.psum(jnp.sum(grad_share * grad_share), ('section', 'dp'))  99.8 us
    ppermute x46, waiting for transfers between devices, shifted(): return lax.ppermute(x, axis, pairs)  85.2 us
    dot_general x33, matrix products, contract_last(): lax.dot_general(lhs_array, rhs_array, (((1,), (1,)), ((), ())), preferred...  61 us
    another operation x1, loops' own time, shards(): lax.fori_loop(0, tick_count, forward_tick, (zero_model, buffer_model, buf...  47.6 us
  transfers between devices with their start and end apart: 49, of which 49 were waited for; matrix products, arithmetic and copies ran while one was open for 5% of the time, Pallas kernels for 0%

commit v1 on v0

v1 whole, which is shorter than its diff:
```python
import functools

import jax
import jax.numpy as jnp
from jax import lax
from jax.experimental import pallas as pl
from jax.experimental.pallas import tpu as pltpu
from jax.sharding import PartitionSpec as P

eps_norm = 1e-05
beta_one = 0.9
beta_two = 0.95
eps_adam = 1e-08
learn_rate = 0.002
decay_rate = 0.1

MESH = pl.DeviceIdType.MESH
WIDTH = 4096
HID = 128
ROWS = 256
TOK = 16
SECTIONS = 8
SHARD = 64
NZ = 16
NX = 4
NY = 4
f32 = jnp.float32
bf16 = jnp.bfloat16


class Place:

    def __init__(self):
        self.s = lax.axis_index("section")
        self.d = lax.axis_index("dp")
        self.c = lax.rem(self.s, 2)
        self.y = self.s // 2
        self.z = self.d // NX
        self.x = lax.rem(self.d, NX)

    def at_z(self, k):
        return (self.s, lax.rem(self.z + k + 2 * NZ, NZ) * NX + self.x)

    def at_x(self, k):
        return (self.s, self.z * NX + lax.rem(self.x + k + NX, NX))

    def at_y(self, k):
        return (lax.rem(self.y + k + NY, NY) * 2 + self.c, self.d)

    def sibling(self):
        return (self.y * 2 + 1 - self.c, self.d)


def greet(partners):
    barrier = pltpu.get_barrier_semaphore()
    for partner in partners:
        pl.semaphore_signal(barrier, inc=1, device_id=partner, device_id_type=MESH)
    pl.semaphore_wait(barrier, len(partners))


def remote(src, dst, send, recv, to):
    return pltpu.make_async_remote_copy(
        src_ref=src, dst_ref=dst, send_sem=send, recv_sem=recv, device_id=to, device_id_type=MESH
    )


def ring_gather(me, block, rz, zs, zr, xzs, xzr, xs, xr, fs, fr, done):
    rx = SHARD - rz

    def zblock(z):
        return block(z, None, 0, rz)

    def xblock(z, x):
        return block(z, x, rz, rx)

    def zcopy(flow, k, mode):
        z = lax.rem(me.z - (k - 1) + 2 * NZ, NZ) if flow == 0 else lax.rem(me.z + (k - 1), NZ)
        part = zblock(z) if mode == 0 else xblock(z, me.x)
        return remote(part, part, zs.at[flow, k, mode], zr.at[flow, k, mode], me.at_z(1 if flow == 0 else -1))

    def xcopy(flow, k, side):
        z = lax.rem(me.z - k + 2 * NZ, NZ) if flow == 0 else lax.rem(me.z + k, NZ)
        part = xblock(z, me.x)
        return remote(part, part, xs.at[flow, k, side], xr.at[flow, k, side], me.at_x(1 if side == 0 else -1))

    def fcopy(flow, k):
        z = lax.rem(me.z - k + 2 * NZ, NZ) if flow == 0 else lax.rem(me.z + k, NZ)
        came = -1 if flow == 0 else 1
        part = xblock(z, lax.rem(me.x + came + NX, NX))
        return remote(part, part, fs.at[flow, k], fr.at[flow, k], me.at_x(-came))

    def first(dx):
        part = block(me.z, me.x, 0, rz)
        return remote(part, part, xzs.at[dx], xzr.at[dx], me.at_x(dx))

    for flow in range(2):
        zcopy(flow, 1, 1).start()
    for dx in range(1, NX):
        first(dx).start()
    for side in range(2):
        xcopy(0, 0, side).start()
    for dx in range(1, NX):
        first(dx).wait_recv()
    for flow in range(2):
        zcopy(flow, 1, 0).start()

    def stage_a(flow, k):
        for mode in (1, 0):
            zcopy(flow, k, mode).wait_recv()

            @pl.when(k < (8 if flow == 0 else 7))
            def _():
                zcopy(flow, k + 1, mode).start()

            if mode == 1:
                for side in range(2):
                    xcopy(flow, k, side).start()

    def stage_b(flow, k):
        for side in range(2):
            xcopy(flow, k, side).wait_recv()
        fcopy(flow, k).start()

    def stage_c(flow, k):
        fcopy(flow, k).wait_recv()
        done(flow, k)

    def step(k, carry):
        stage_a(0, k)

        @pl.when(k < 8)
        def _():
            stage_a(1, k)

        stage_b(0, k - 1)

        @pl.when(k > 1)
        def _():
            stage_b(1, k - 1)
            stage_c(0, k - 2)

        @pl.when(k > 2)
        def _():
            stage_c(1, k - 2)

        return carry

    lax.fori_loop(1, 9, step, 0)
    stage_b(0, 8)
    stage_c(0, 7)
    stage_c(1, 7)
    stage_c(0, 8)

    def drain(k, carry):
        for flow in range(2):

            @pl.when((k >= 1) & (k <= (8 if flow == 0 else 7)))
            def _():
                for mode in range(2):
                    zcopy(flow, k, mode).wait_send()

            @pl.when((k <= (8 if flow == 0 else 7)) & (k >= flow))
            def _():
                for side in range(2):
                    xcopy(flow, k, side).wait_send()
                fcopy(flow, k).wait_send()

        return carry

    lax.fori_loop(0, 9, drain, 0)
    for dx in range(1, NX):
        first(dx).wait_send()


GATHER_SEMS = [
    pltpu.SemaphoreType.DMA((2, 9, 2)),
    pltpu.SemaphoreType.DMA((2, 9, 2)),
    pltpu.SemaphoreType.DMA((NX,)),
    pltpu.SemaphoreType.DMA((NX,)),
    pltpu.SemaphoreType.DMA((2, 9, 2)),
    pltpu.SemaphoreType.DMA((2, 9, 2)),
    pltpu.SemaphoreType.DMA((2, 9)),
    pltpu.SemaphoreType.DMA((2, 9)),
]


def gather_all_kernel(w_ref, gain_ref, all_ref, gains_ref, ys, yr, gs, gr, ss, sr, own, *ring_sems):
    me = Place()
    greet(
        [me.at_y(k) for k in range(1, NY)]
        + [me.at_x(k) for k in range(1, NX)]
        + [me.at_z(1), me.at_z(-1), me.sibling()]
    )

    def ycopy(k):
        return remote(w_ref, all_ref.at[me.c, me.y, me.z, me.x], ys.at[k], yr.at[k], me.at_y(k))

    def gcopy(k):
        part = gains_ref.at[me.c, me.y]
        return remote(gain_ref, part, gs.at[k], gr.at[k], me.at_y(k))

    for k in range(1, NY):
        ycopy(k).start()
        gcopy(k).start()
    keep = pltpu.make_async_copy(w_ref, all_ref.at[me.c, me.y, me.z, me.x], own.at[0])
    keep_gain = pltpu.make_async_copy(gain_ref, gains_ref.at[me.c, me.y], own.at[1])
    keep.start()
    keep_gain.start()
    for k in range(1, NY):
        ycopy(k).wait_recv()
        gcopy(k).wait_recv()
    keep.wait()
    keep_gain.wait()
    gains = remote(gains_ref.at[me.c], gains_ref.at[me.c], ss.at[2, 0], sr.at[2, 0], me.sibling())
    gains.start()

    def block(z, x, lo, n):
        if x is None:
            return all_ref.at[me.c, :, z, :, pl.ds(lo, n), :]
        return all_ref.at[me.c, :, z, x, pl.ds(lo, n), :]

    def side_copy(flow, k):
        z = lax.rem(me.z - k + 2 * NZ, NZ) if flow == 0 else lax.rem(me.z + k, NZ)
        part = all_ref.at[me.c, :, z]
        return remote(part, part, ss.at[flow, k], sr.at[flow, k], me.sibling())

    ring_gather(me, block, 32, *ring_sems, lambda flow, k: side_copy(flow, k).start())

    def finish(k, carry):
        for flow in range(2):

            @pl.when((k >= flow) & (k <= (8 if flow == 0 else 7)))
            def _():
                side_copy(flow, k).wait()

        return carry

    lax.fori_loop(0, 9, finish, 0)
    gains.wait()
    for k in range(1, NY):
        ycopy(k).wait_send()
        gcopy(k).wait_send()


def gather_all(shard, gain_tile):
    return pl.pallas_call(
        gather_all_kernel,
        out_shape=(
            jax.ShapeDtypeStruct((2, NY, NZ, NX, SHARD, 2 * HID), bf16),
            jax.ShapeDtypeStruct((2, NY, 8, 128), f32),
        ),
        in_specs=[pl.BlockSpec(memory_space=pltpu.VMEM)] * 2,
        out_specs=(pl.BlockSpec(memory_space=pl.ANY), pl.BlockSpec(memory_space=pltpu.VMEM)),
        scratch_shapes=[
            pltpu.SemaphoreType.DMA((NY,)),
            pltpu.SemaphoreType.DMA((NY,)),
            pltpu.SemaphoreType.DMA((NY,)),
            pltpu.SemaphoreType.DMA((NY,)),
            pltpu.SemaphoreType.DMA((3, 9)),
            pltpu.SemaphoreType.DMA((3, 9)),
            pltpu.SemaphoreType.DMA((2,)),
            *GATHER_SEMS,
        ],
        compiler_params=pltpu.CompilerParams(collective_id=0, has_side_effects=True),
        name="gather_all",
    )(shard, gain_tile)


def normalize(values):
    centred = values - jnp.mean(values, axis=-1, keepdims=True)
    inv_spread = lax.rsqrt(jnp.mean(centred * centred, axis=-1, keepdims=True) + eps_norm)
    return (centred * inv_spread, inv_spread)


def contract_last(lhs_array, rhs_array):
    return lax.dot_general(
        lhs_array, rhs_array, (((1,), (1,)), ((), ())), preferred_element_type=f32
    )


def contract_first(lhs_array, rhs_array):
    return lax.dot_general(
        lhs_array, rhs_array, (((0,), (0,)), ((), ())), preferred_element_type=f32
    )


root_two_over_pi = 0.7978845608028654
cubic = 0.044715


def gelu_parts(v):
    t = jnp.tanh(root_two_over_pi * (v + cubic * (v * v * v)))
    cdf = 0.5 * (1.0 + t)
    slope = cdf + 0.5 * v * (1.0 - t * t) * (root_two_over_pi * (1.0 + 3.0 * cubic * v * v))
    return v * cdf, slope


CHUNK = 256


def relay_kernel(
    which_ref, x_hbm, all_hbm, gains_ref, valid_ref, grad_ref, probe_ref,
    w, x, g, nb, inv, pre, hid, out_b, wsum, w_sem, x_sem,
):
    mine = lax.axis_index("section")

    def load(s):
        return pltpu.make_async_copy(all_hbm.at[lax.rem(s, 2), s // 2], w.at[s], w_sem.at[s])

    get_x = pltpu.make_async_copy(x_hbm, x, x_sem)
    get_x.start()
    for s in range(SECTIONS):
        load(s).start()
    get_x.wait()

    def gain_of(s):
        return gains_ref[lax.rem(s, 2), s // 2, 0:1, 0:1]

    def forward(s, carry):
        @pl.when(s == mine)
        def _():
            start = pl.multiple_of(which_ref[0] * TOK, TOK)
            probe_ref[...] = x[pl.ds(start, TOK), :]

        def norm_rows(i, carry):
            rows = pl.ds(pl.multiple_of(i * 16, 16), 16)
            normed, spread = normalize(x[rows, :].astype(f32))
            nb[s, rows, :] = normed.astype(bf16)
            inv[s, rows, :] = jnp.broadcast_to(spread, (16, 128))
            return carry

        lax.fori_loop(0, ROWS // 16, norm_rows, 0)
        load(s).wait()
        pre_act = jnp.dot(nb[s], w[s, :, :HID], preferred_element_type=f32)
        pre[s] = pre_act
        hidden = gelu_parts(pre_act)[0].astype(bf16)
        hid[s] = hidden
        gain = gain_of(s)

        def columns(j, total):
            cols = pl.ds(pl.multiple_of(j * CHUNK, CHUNK), CHUNK)
            branch = contract_last(hidden, w[s, cols, HID:])
            x[:, cols] = (x[:, cols].astype(f32) + gain * branch).astype(bf16)
            return total + jnp.sum(w[s, cols, :HID].astype(f32), axis=0, keepdims=True)

        wsum[s] = lax.fori_loop(0, WIDTH // CHUNK, columns, jnp.zeros((1, HID), f32))
        return carry

    lax.fori_loop(0, SECTIONS, forward, 0)
    keep = valid_ref[:, 0:1] > 0.5

    def mask(j, carry):
        cols = pl.ds(pl.multiple_of(j * CHUNK, CHUNK), CHUNK)
        g[:, cols] = jnp.where(keep, x[:, cols].astype(f32), 0.0).astype(bf16)
        return carry

    lax.fori_loop(0, WIDTH // CHUNK, mask, 0)

    def inner_grads(s):
        gain = gain_of(s)

        def columns(j, total):
            cols = pl.ds(pl.multiple_of(j * CHUNK, CHUNK), CHUNK)
            out = (gain * g[:, cols].astype(f32)).astype(bf16)
            out_b[:, cols] = out
            return total + jnp.dot(out, w[s, cols, HID:], preferred_element_type=f32)

        hidden_grad = lax.fori_loop(0, WIDTH // CHUNK, columns, jnp.zeros((ROWS, HID), f32))
        return (gelu_parts(pre[s])[1] * hidden_grad).astype(bf16)

    def backward(i, carry):
        s = SECTIONS - 1 - i
        pre_b = inner_grads(s)
        pre_f = pre_b.astype(f32)
        grad_mean = jnp.sum(pre_f * wsum[s], axis=-1, keepdims=True) * (1.0 / WIDTH)
        cross_mean = jnp.sum(pre_f * pre[s], axis=-1, keepdims=True) * (1.0 / WIDTH)
        spread = inv[s, :, 0:1]

        def columns(j, carry):
            cols = pl.ds(pl.multiple_of(j * CHUNK, CHUNK), CHUNK)
            normed_grad = contract_last(pre_b, w[s, cols, :HID])
            normed = nb[s, :, cols].astype(f32)
            g[:, cols] = (
                g[:, cols].astype(f32) + spread * (normed_grad - grad_mean - normed * cross_mean)
            ).astype(bf16)
            return carry

        lax.fori_loop(0, WIDTH // CHUNK, columns, 0)
        return carry

    lax.fori_loop(0, SECTIONS - 1 - mine, backward, 0)
    pre_b = inner_grads(mine)
    hidden = hid[mine]

    def columns(j, carry):
        cols = pl.ds(pl.multiple_of(j * CHUNK, CHUNK), CHUNK)
        grad_ref[cols, :HID] = contract_first(pre_b, nb[mine, :, cols]).T.astype(bf16)
        grad_ref[cols, HID:] = contract_first(hidden, out_b[:, cols]).T.astype(bf16)
        return carry

    lax.fori_loop(0, WIDTH // CHUNK, columns, 0)


def relay(which, rows, all_weights, gains, valid):
    return pl.pallas_call(
        relay_kernel,
        out_shape=(
            jax.ShapeDtypeStruct((WIDTH, 2 * HID), bf16),
            jax.ShapeDtypeStruct((TOK, WIDTH), bf16),
        ),
        in_specs=[
            pl.BlockSpec(memory_space=pltpu.SMEM),
            pl.BlockSpec(memory_space=pl.ANY),
            pl.BlockSpec(memory_space=pl.ANY),
            pl.BlockSpec(memory_space=pltpu.VMEM),
            pl.BlockSpec(memory_space=pltpu.VMEM),
        ],
        out_specs=(
            pl.BlockSpec(memory_space=pltpu.VMEM),
            pl.BlockSpec(memory_space=pltpu.VMEM),
        ),
        scratch_shapes=[
            pltpu.VMEM((SECTIONS, WIDTH, 2 * HID), bf16),
            pltpu.VMEM((ROWS, WIDTH), bf16),
            pltpu.VMEM((ROWS, WIDTH), bf16),
            pltpu.VMEM((SECTIONS, ROWS, WIDTH), bf16),
            pltpu.VMEM((SECTIONS, ROWS, 128), f32),
            pltpu.VMEM((SECTIONS, ROWS, HID), f32),
            pltpu.VMEM((SECTIONS, ROWS, HID), bf16),
            pltpu.VMEM((ROWS, WIDTH), bf16),
            pltpu.VMEM((SECTIONS, 1, HID), f32),
            pltpu.SemaphoreType.DMA((SECTIONS,)),
            pltpu.SemaphoreType.DMA,
        ],
        compiler_params=pltpu.CompilerParams(vmem_limit_bytes=58 * 2**20),
        name="relay",
    )(which, rows, all_weights, gains, valid)


HALF = SHARD // 2
GROUP = SECTIONS * NX


def finish_kernel(
    grad_ref, master_ref, first_ref, second_ref, gain_ref, probe_ref,
    out_ref, new_master_ref, new_first_ref, new_second_ref,
    fresh, ra, rb, xa, xa_out, xb, tb, share, near, far,
    zs, zr, xs, xr, ns, nr, ms, mr, *ring_sems,
):
    me = Place()

    def group_at(i):
        ds, dx = i // NX, lax.rem(i, NX)
        return (lax.rem(me.s + ds, SECTIONS), me.z * NX + lax.rem(me.x + dx, NX))

    greet([group_at(i) for i in range(1, GROUP)] + [me.at_z(k) for k in range(1, NZ)])

    def target_z(flow, k):
        if flow == 0:
            return lax.rem(me.z + 9 - k, NZ)
        return lax.rem(me.z - 8 + k + NZ, NZ)

    def zcopy(flow, k, mode, first=False):
        to = me.at_z(1 if flow == 0 else -1)
        send, recv = zs.at[flow, k, mode], zr.at[flow, k, mode]
        if mode == 0:
            src = grad_ref.at[target_z(flow, k), :, pl.ds(0, HALF), :] if first else ra.at[flow, k - 1]
            return remote(src, ra.at[flow, k], send, recv, to)
        src = tb.at[target_z(flow, k)] if first else rb.at[flow, k - 1]
        return remote(src, rb.at[flow, k], send, recv, to)

    def xbcopy(dx):
        src = grad_ref.at[:, lax.rem(me.x + dx, NX), pl.ds(HALF, HALF), :]
        return remote(src, xb.at[dx], xs.at[1, dx], xr.at[1, dx], me.at_x(dx))

    def xacopy(dx):
        src = xa_out.at[lax.rem(me.x + dx, NX)]
        return remote(src, xa.at[dx], xs.at[0, dx], xr.at[0, dx], me.at_x(dx))

    for flow in range(2):
        zcopy(flow, 1, 0, True).start()
    for dx in range(1, NX):
        xbcopy(dx).start()

    def step_a(flow, k):
        zcopy(flow, k, 0).wait_recv()

        @pl.when(k < (8 if flow == 0 else 7))
        def _():
            own = grad_ref[target_z(flow, k + 1), :, pl.ds(0, HALF), :].astype(f32)
            ra[flow, k] = (ra[flow, k].astype(f32) + own).astype(bf16)
            zcopy(flow, k + 1, 0).start()

    def step_b(flow, k):
        zcopy(flow, k, 1).wait_recv()

        @pl.when(k < (8 if flow == 0 else 7))
        def _():
            rb[flow, k] = (rb[flow, k].astype(f32) + tb[target_z(flow, k + 1)].astype(f32)).astype(bf16)
            zcopy(flow, k + 1, 1).start()

    def begin_b():
        for dx in range(1, NX):
            xbcopy(dx).wait_recv()

        def add(z, carry):
            total = grad_ref[z, me.x, pl.ds(HALF, HALF), :].astype(f32)
            for dx in range(1, NX):
                total = total + xb[dx, z].astype(f32)
            tb[z] = total.astype(bf16)
            return carry

        lax.fori_loop(0, NZ, add, 0)
        for flow in range(2):
            zcopy(flow, 1, 1, True).start()

    def ring(k, carry):
        @pl.when(k <= 8)
        def _():
            step_a(0, k)

        @pl.when(k <= 7)
        def _():
            step_a(1, k)

        @pl.when(k == 3)
        def _():
            begin_b()

        @pl.when(k == 8)
        def _():
            def total(x, carry):
                block = (
                    grad_ref[me.z, x, pl.ds(0, HALF), :].astype(f32)
                    + ra[0, 8, x].astype(f32)
                    + ra[1, 7, x].astype(f32)
                )
                xa_out[x] = block.astype(bf16)
                return carry

            lax.fori_loop(0, NX, total, 0)
            for dx in range(1, NX):
                xacopy(dx).start()

        @pl.when(k > 3)
        def _():
            step_b(0, k - 3)

        @pl.when((k > 3) & (k < 11))
        def _():
            step_b(1, k - 3)

        return carry

    lax.fori_loop(1, 12, ring, 0)
    share[pl.ds(HALF, HALF), :] = tb[me.z].astype(f32) + rb[0, 8].astype(f32) + rb[1, 7].astype(f32)
    for dx in range(1, NX):
        xacopy(dx).wait_recv()
    total = xa_out[me.x].astype(f32)
    for dx in range(1, NX):
        total = total + xa[dx].astype(f32)
    share[pl.ds(0, HALF), :] = total

    squares = jnp.zeros((8, 128), f32)
    for i in range(SHARD // 8):
        for j in range(2):
            tile = share[pl.ds(i * 8, 8), pl.ds(j * 128, 128)]
            squares = squares + tile * tile
    near[0] = squares

    def ncopy(i):
        return remote(near.at[0], near.at[i], ns.at[i], nr.at[i], group_at(i))

    def mcopy(k):
        return remote(far.at[0], far.at[k], ms.at[k], mr.at[k], me.at_z(k))

    def n_start(i, carry):
        ncopy(i).start()
        return carry

    def n_wait(i, carry):
        ncopy(i).wait()
        return carry

    def m_start(i, carry):
        mcopy(i).start()
        return carry

    def m_wait(i, carry):
        mcopy(i).wait()
        return carry

    lax.fori_loop(1, GROUP, n_start, 0)
    lax.fori_loop(1, GROUP, n_wait, 0)
    far[0] = jnp.sum(near[...], axis=0)
    lax.fori_loop(1, NZ, m_start, 0)
    lax.fori_loop(1, NZ, m_wait, 0)
    norm_sq = jnp.sum(jnp.sum(far[...], axis=0), keepdims=True)
    clip_factor = 1.0 / jnp.maximum(jnp.sqrt(norm_sq), 1.0)
    clipped = share[...] * clip_factor
    master_now = master_ref[...]
    new_first = beta_one * first_ref[...] + (1.0 - beta_one) * clipped
    new_second = beta_two * second_ref[...] + (1.0 - beta_two) * clipped * clipped
    new_master = master_now - learn_rate * (
        new_first / (jnp.sqrt(new_second) + eps_adam) + decay_rate * master_now
    )
    fresh[me.z, me.x] = new_master.astype(bf16)
    new_master_ref[...] = new_master
    new_first_ref[...] = new_first
    new_second_ref[...] = new_second

    def block(z, x, lo, n):
        if x is None:
            return fresh.at[z, :, pl.ds(lo, n), :]
        return fresh.at[z, x, pl.ds(lo, n), :]

    ring_gather(me, block, HALF, *ring_sems, lambda flow, k: None)

    def drain(k, carry):
        for flow in range(2):

            @pl.when(k <= (8 if flow == 0 else 7))
            def _():
                for mode in range(2):
                    zcopy(flow, k, mode).wait_send()

        return carry

    lax.fori_loop(2, 9, drain, 0)
    for flow in range(2):
        for mode in range(2):
            zcopy(flow, 1, mode, True).wait_send()
    for dx in range(1, NX):
        xbcopy(dx).wait_send()
        xacopy(dx).wait_send()

    values = probe_ref[...].astype(f32)
    normed = normalize(values)[0].astype(bf16)
    pre_act = jnp.zeros((TOK, HID), f32)
    for z in range(NZ):
        part = fresh[z, :, :, :HID].reshape(256, HID)
        pre_act = pre_act + jnp.dot(normed[:, z * 256 : (z + 1) * 256], part, preferred_element_type=f32)
    hidden = gelu_parts(pre_act)[0].astype(bf16)
    gain = gain_ref[0:1, 0:1]
    for z in range(NZ):
        part = fresh[z, :, :, HID:].reshape(256, HID)
        cols = slice(z * 256, (z + 1) * 256)
        out_ref[:, cols] = (values[:, cols] + gain * contract_last(hidden, part)).astype(bf16)


def finish(grad, master, first_moment, second_moment, gain_tile, probe_in):
    state = jax.ShapeDtypeStruct((SHARD, 2 * HID), f32)
    vmem = pl.BlockSpec(memory_space=pltpu.VMEM)
    return pl.pallas_call(
        finish_kernel,
        out_shape=(jax.ShapeDtypeStruct((TOK, WIDTH), bf16), state, state, state),
        in_specs=[vmem] * 6,
        out_specs=(vmem,) * 4,
        scratch_shapes=[
            pltpu.VMEM((NZ, NX, SHARD, 2 * HID), bf16),
            pltpu.VMEM((2, 9, NX, HALF, 2 * HID), bf16),
            pltpu.VMEM((2, 9, HALF, 2 * HID), bf16),
            pltpu.VMEM((NX, HALF, 2 * HID), bf16),
            pltpu.VMEM((NX, HALF, 2 * HID), bf16),
            pltpu.VMEM((NX, NZ, HALF, 2 * HID), bf16),
            pltpu.VMEM((NZ, HALF, 2 * HID), bf16),
            pltpu.VMEM((SHARD, 2 * HID), f32),
            pltpu.VMEM((GROUP, 8, 128), f32),
            pltpu.VMEM((NZ, 8, 128), f32),
            pltpu.SemaphoreType.DMA((2, 9, 2)),
            pltpu.SemaphoreType.DMA((2, 9, 2)),
            pltpu.SemaphoreType.DMA((2, NX)),
            pltpu.SemaphoreType.DMA((2, NX)),
            pltpu.SemaphoreType.DMA((GROUP,)),
            pltpu.SemaphoreType.DMA((GROUP,)),
            pltpu.SemaphoreType.DMA((NZ,)),
            pltpu.SemaphoreType.DMA((NZ,)),
            *GATHER_SEMS,
        ],
        compiler_params=pltpu.CompilerParams(
            collective_id=1, has_side_effects=True, vmem_limit_bytes=40 * 2**20
        ),
        name="finish",
    )(grad, master, first_moment, second_moment, gain_tile, probe_in)


def shards(inputs, stashed, master, first_moment, second_moment, counts, plan, layer_index):
    gain_tile = jnp.full((8, 128), lax.rsqrt(1.0 + layer_index.astype(f32) / 8.0)[0], f32)
    all_weights, gains = gather_all(stashed[0], gain_tile)
    row_pos = lax.broadcasted_iota(jnp.int32, (16, TOK), 1)
    valid = (row_pos < counts[0][:, None]).astype(f32).reshape(ROWS, 1)
    grad, probe_in = relay(
        plan[15:],
        inputs.reshape(ROWS, WIDTH),
        all_weights.reshape(2, NY, WIDTH, 2 * HID),
        gains,
        jnp.broadcast_to(valid, (ROWS, 128)),
    )
    probe_out, new_master, new_first, new_second = finish(
        grad.reshape(NZ, NX, SHARD, 2 * HID), master[0], first_moment[0], second_moment[0], gain_tile, probe_in
    )
    return (probe_out[None], new_master[None], new_first[None], new_second[None])


def solution(mesh):
    in_specs = (
        P(None, "dp", None),
        P("section", "dp", None),
        P("section", "dp", None),
        P("section", "dp", None),
        P("section", "dp", None),
        P("dp", None),
        P(),
        P("section"),
    )
    out_specs = (
        P("section", "dp", None),
        P("section", "dp", None),
        P("section", "dp", None),
        P("section", "dp", None),
    )
    return jax.shard_map(shards, mesh=mesh, in_specs=in_specs, out_specs=out_specs, check_vma=False)
```

time: 1740 us -> 333 us (0.19)
  waiting for transfers between devices: 1080 us -> 0 us
  Pallas kernels: 0 us -> 323 us
  other arithmetic: 151 us -> 0.73 us
  starting transfers between devices: 147 us -> 0 us
  matrix products: 121 us -> 0 us
  blocking collectives: 99.8 us -> 0 us
  local copies, waits for them, and re-layouts: 67.5 us -> 7.73 us
  loops' own time: 49.3 us -> 0 us
    unnamed x4 -> x0, waiting for transfers between devices: 716 us -> none
    pallas_call x0 -> x3, Pallas kernels: none -> 323 us  [the longest x1 141 us: finish(): pl.pallas_call(finish_kernel, out_shape=(jax.ShapeDtypeStruct((TOK, WIDTH...]
    all_gather x2 -> x0, waiting for transfers between devices: 281 us -> none  [fetch_rows(): return lax.all_gather(shard_rows, 'dp', axis=0, tiled=True)]
    ppermute x46 -> x0, starting transfers between devices: 146 us -> none  [shifted(): return lax.ppermute(x, axis, pairs)]
    dot_general x67 -> x0, matrix products: 121 us -> none  [the longest x33 61 us: contract_last(): lax.dot_general(lhs_array, rhs_array, (((1,), (1,)), ((), ())), preferred...]
    psum x1 -> x0, blocking collectives: 99.8 us -> none  [shards(): norm_sq = lax.psum(jnp.sum(grad_share * grad_share), ('section', 'dp'))]
    ppermute x46 -> x0, waiting for transfers between devices: 85.2 us -> none  [shifted(): return lax.ppermute(x, axis, pairs)]
    another operation x48 -> x0, loops' own time: 49.3 us -> none  [the longest x1 47.6 us: shards(): lax.fori_loop(0, tick_count, forward_tick, (zero_model, buffer_model, buf...]
  transfers between devices with their start and end apart: 49 -> 0, of which waited for: 49 -> 0; matrix products, arithmetic and copies ran while one was open for 5% -> 0% of each run, Pallas kernels for 0% -> 0%
where the time goes in v1:
time: 333 us
  Pallas kernels  323 us (97%)
  local copies, waits for them, and re-layouts  7.73 us (2%)
    pallas_call x1, Pallas kernels, finish(): pl.pallas_call(finish_kernel, out_shape=(jax.ShapeDtypeStruct((TOK, WIDTH...  141 us
    pallas_call x1, Pallas kernels, gather_all(): pl.pallas_call(gather_all_kernel, out_shape=(jax.ShapeDtypeStruct((2, NY,...  92.3 us
    pallas_call x1, Pallas kernels, relay(): pl.pallas_call(relay_kernel, out_shape=(jax.ShapeDtypeStruct((WIDTH, 2 *...  89.4 us

profile of v1, /device:TPU:24, one launch (start us, length us, event | category | flops | bytes accessed | tf_op | source)
XLA Modules:
  0.0 333.0 jit_solution(18099057913795642063)
XLA Ops:
  1.3 1.2 slice.3.which_ref
  2.6 0.6 broadcast_in_dim.20.gain_ref
  3.1 0.7 fusion
  3.9 0.1 reshape.39
  4.0 0.8 broadcast_in_dim.21.valid_ref
  4.7 92.3 %gather_all.1 = (bf16[2,4,16,4,64,256]{5,4,3,2,1,0:T(8,128)(2,1)}, f32[2,4,8,128]{3,2,1,0:T(8,128)}) custom-call(bf16[64,256]{1,0:T(8,128)(2,1)} %bitcast.23, f32[8,128]{1,0:T(8,128)} %broadcast_in_dim.20.gain_ref), custom_call_target="tpu_custom_call" | custom-call | tf_op jit(solution)/shard_map/gather_all/pallas_call | solution.py:246
  97.1 0.0 copy-start.2
  97.1 0.0 copy-start.3
  97.1 0.0 copy-start.4
  97.1 0.0 copy-start.5
  97.1 89.4 %relay.1 = (bf16[4096,256]{1,0:T(8,128)(2,1)}, bf16[16,4096]{1,0:T(8,128)(2,1)}) custom-call(s32[1]{0:T(128)} %slice.3.which_ref, bf16[256,4096]{1,0:T(8,128)(2,1)} %bitcast.22, bf16[2,4,4096,256]{3,2,1,0:T(8,128)(2,1)} %bitcast.21, f32[2,4,8,128]{3,2,1,0:T(8,128)} %get-tuple-element.13.gains_ref, f32[256,128]{1,0:T(8,128)} %broadcast_in_dim.21.valid_ref), custom_call_target="tpu_custom_call" | custom-call | tf_op jit(solution)/shard_map/relay/pallas_call | solution.py:405
  186.6 0.0 copy-done.2
  186.6 0.0 copy-done.3
  186.6 0.0 copy-done.4
  186.6 0.0 copy-done.5
  186.6 0.0 copy-start
  186.6 1.6 copy-done
  188.2 0.0 copy-start.1
  188.2 0.9 copy-done.1
  189.1 141.3 %finish.1 = (bf16[16,4096]{1,0:T(8,128)(2,1)S(1)}, f32[64,256]{1,0:T(8,128)S(1)}, f32[64,256]{1,0:T(8,128)S(1)}, f32[64,256]{1,0:T(8,128)S(1)}) custom-call(bf16[16,4,64,256]{3,2,1,0:T(8,128)(2,1)S(1)} %bitcast.13, f32[64,256]{1,0:T(8,128)S(1)} %bitcast.15, f32[64,256]{1,0:T(8,128)S(1)} %bitcast.16, f32[64,256]{1,0:T(8,128)S(1)} %bitcast.17, ...), custom_call_target="tpu_custom_call" | custom-call | tf_op jit(solution)/shard_map/finish/pallas_call | solution.py:654
  330.4 0.7 copy.17
  331.1 0.6 copy.18
  331.7 0.6 copy.19
  332.3 0.6 copy.20
Async XLA Ops:
  97.1 89.5 %copy-start.2 = (f32[1,64,256]{2,1,0:T(8,128)S(1)}, f32[1,64,256]{2,1,0:T(8,128)}, u32[]{:S(2)}) copy-start(f32[1,64,256]{2,1,0:T(8,128)} %param.10) | copy-start | bytes 196612
  97.1 89.5 %copy-start.3 = (f32[1,64,256]{2,1,0:T(8,128)S(1)}, f32[1,64,256]{2,1,0:T(8,128)}, u32[]{:S(2)}) copy-start(f32[1,64,256]{2,1,0:T(8,128)} %param.11) | copy-start | bytes 196612
  97.1 89.5 %copy-start.4 = (f32[1,64,256]{2,1,0:T(8,128)S(1)}, f32[1,64,256]{2,1,0:T(8,128)}, u32[]{:S(2)}) copy-start(f32[1,64,256]{2,1,0:T(8,128)} %param.12) | copy-start | bytes 196612
  97.1 89.5 %copy-start.5 = (f32[8,128]{1,0:T(8,128)S(1)}, f32[8,128]{1,0:T(8,128)}, u32[]{:S(2)}) copy-start(f32[8,128]{1,0:T(8,128)} %broadcast_in_dim.20.gain_ref) | copy-start | bytes 12292
  186.6 1.6 copy-start
  188.2 0.9 copy-start.1

commit v2 on v1

--- a/solution.py
+++ b/solution.py
@@ -295,113 +295,209 @@
     return v * cdf, slope
 
 
-CHUNK = 256
+OWN = ROWS // 2
+CHUNK = 512
+CHUNKS = WIDTH // CHUNK
+PIECES = 4
+PIECE = WIDTH // PIECES
+
+
+def tiled(a):
+    return jnp.concatenate([a] * (CHUNK // 128), axis=1)
+
+
+def folded(a):
+    total = a[:, 0:128]
+    for i in range(1, a.shape[1] // 128):
+        total = total + a[:, i * 128 : (i + 1) * 128]
+    return total
+
+
+def row_mean(a):
+    return jnp.broadcast_to(jnp.sum(a, axis=-1, keepdims=True) * (1.0 / WIDTH), (OWN, 128))
 
 
 def relay_kernel(
-    which_ref, x_hbm, all_hbm, gains_ref, valid_ref, grad_ref, probe_ref,
-    w, x, g, nb, inv, pre, hid, out_b, wsum, w_sem, x_sem,
+    x_hbm, all_hbm, gains_ref, valid_ref, grad_ref, probe_ref,
+    w, x, g, cb, inv, pre, hid, wsum, out, pg, cb_in, hid_in, out_in, pg_in, pr, pr_in,
+    w_sem, x_sem, fs, fr, bs, br,
 ):
-    mine = lax.axis_index("section")
+    me = Place()
+    mine = me.s
+    sib = me.y * 2 + 1 - me.c
+    greet([me.sibling()])
 
     def load(s):
         return pltpu.make_async_copy(all_hbm.at[lax.rem(s, 2), s // 2], w.at[s], w_sem.at[s])
 
-    get_x = pltpu.make_async_copy(x_hbm, x, x_sem)
+    get_x = pltpu.make_async_copy(
+        x_hbm.at[pl.ds(pl.multiple_of(me.c * OWN, OWN), OWN)], x, x_sem
+    )
     get_x.start()
     for s in range(SECTIONS):
         load(s).start()
     get_x.wait()
 
+    def send_cb():
+        return remote(cb.at[sib], cb_in, fs.at[0], fr.at[0], me.sibling())
+
+    def send_hid():
+        return remote(hid.at[sib], hid_in, fs.at[1], fr.at[1], me.sibling())
+
+    def send_pr():
+        return remote(pr, pr_in, fs.at[2], fr.at[2], me.sibling())
+
+    def send_out(p):
+        cols = pl.ds(p * PIECE, PIECE)
+        return remote(out.at[1 - me.c, :, cols], out_in.at[:, cols], bs.at[p], br.at[p], me.sibling())
+
+    def send_pg():
+        return remote(pg.at[1 - me.c], pg_in, bs.at[PIECES], br.at[PIECES], me.sibling())
+
     def gain_of(s):
-        return gains_ref[lax.rem(s, 2), s // 2, 0:1, 0:1]
-
-    def forward(s, carry):
+        return gains_ref[lax.rem(s, 2), s // 2, 0:1, :]
+
+    def cols_of(j):
+        return slice(j * CHUNK, (j + 1) * CHUNK)
+
+    def picked(ref):
+        for j in range(CHUNKS):
+            cols = cols_of(j)
+            rows = jnp.zeros((TOK, CHUNK), f32)
+            for i in range(OWN // TOK):
+                part = pl.ds(i * TOK, TOK)
+                chosen = valid_ref[1, pl.ds(pl.multiple_of(me.c * OWN + i * TOK, TOK), TOK), :]
+                rows = rows + tiled(chosen) * x[part, cols].astype(f32)
+            ref[:, cols] = rows.astype(bf16)
+
+    total = jnp.zeros((OWN, 128), f32)
+    for j in range(CHUNKS):
+        total = total + folded(x[:, cols_of(j)].astype(f32))
+
+    def forward(s, total):
         @pl.when(s == mine)
         def _():
-            start = pl.multiple_of(which_ref[0] * TOK, TOK)
-            probe_ref[...] = x[pl.ds(start, TOK), :]
-
-        def norm_rows(i, carry):
-            rows = pl.ds(pl.multiple_of(i * 16, 16), 16)
-            normed, spread = normalize(x[rows, :].astype(f32))
-            nb[s, rows, :] = normed.astype(bf16)
-            inv[s, rows, :] = jnp.broadcast_to(spread, (16, 128))
-            return carry
-
-        lax.fori_loop(0, ROWS // 16, norm_rows, 0)
+            picked(probe_ref)
+
+        @pl.when(s == sib)
+        def _():
+            picked(pr)
+            send_pr().start()
+
         load(s).wait()
-        pre_act = jnp.dot(nb[s], w[s, :, :HID], preferred_element_type=f32)
+        mean = tiled(row_mean(total))
+        squares = jnp.zeros((OWN, 128), f32)
+        acc = jnp.zeros((OWN, HID), f32)
+        columns = jnp.zeros((8, 128), f32)
+        for j in range(CHUNKS):
+            cols = cols_of(j)
+            centred = x[:, cols].astype(f32) - mean
+            squares = squares + folded(centred * centred)
+            low = centred.astype(bf16)
+            cb[s, :, cols] = low
+            part = w[s, cols, :HID]
+            acc = acc + jnp.dot(low, part, preferred_element_type=f32)
+            columns = columns + jnp.sum(part.astype(f32).reshape(CHUNK // 8, 8, HID), axis=0)
+        wsum[s] = columns
+        spread = lax.rsqrt(row_mean(squares) + eps_norm)
+        inv[s] = spread
+        pre_act = acc * spread
         pre[s] = pre_act
         hidden = gelu_parts(pre_act)[0].astype(bf16)
         hid[s] = hidden
-        gain = gain_of(s)
-
-        def columns(j, total):
-            cols = pl.ds(pl.multiple_of(j * CHUNK, CHUNK), CHUNK)
+
+        @pl.when(s == sib)
+        def _():
+            send_cb().start()
+            send_hid().start()
+
+        gain = tiled(gain_of(s))
+        total = jnp.zeros((OWN, 128), f32)
+        for j in range(CHUNKS):
+            cols = cols_of(j)
             branch = contract_last(hidden, w[s, cols, HID:])
-            x[:, cols] = (x[:, cols].astype(f32) + gain * branch).astype(bf16)
-            return total + jnp.sum(w[s, cols, :HID].astype(f32), axis=0, keepdims=True)
-
-        wsum[s] = lax.fori_loop(0, WIDTH // CHUNK, columns, jnp.zeros((1, HID), f32))
-        return carry
-
-    lax.fori_loop(0, SECTIONS, forward, 0)
-    keep = valid_ref[:, 0:1] > 0.5
-
-    def mask(j, carry):
-        cols = pl.ds(pl.multiple_of(j * CHUNK, CHUNK), CHUNK)
-        g[:, cols] = jnp.where(keep, x[:, cols].astype(f32), 0.0).astype(bf16)
-        return carry
-
-    lax.fori_loop(0, WIDTH // CHUNK, mask, 0)
-
-    def inner_grads(s):
-        gain = gain_of(s)
-
-        def columns(j, total):
-            cols = pl.ds(pl.multiple_of(j * CHUNK, CHUNK), CHUNK)
-            out = (gain * g[:, cols].astype(f32)).astype(bf16)
-            out_b[:, cols] = out
-            return total + jnp.dot(out, w[s, cols, HID:], preferred_element_type=f32)
-
-        hidden_grad = lax.fori_loop(0, WIDTH // CHUNK, columns, jnp.zeros((ROWS, HID), f32))
-        return (gelu_parts(pre[s])[1] * hidden_grad).astype(bf16)
-
-    def backward(i, carry):
-        s = SECTIONS - 1 - i
-        pre_b = inner_grads(s)
-        pre_f = pre_b.astype(f32)
-        grad_mean = jnp.sum(pre_f * wsum[s], axis=-1, keepdims=True) * (1.0 / WIDTH)
-        cross_mean = jnp.sum(pre_f * pre[s], axis=-1, keepdims=True) * (1.0 / WIDTH)
-        spread = inv[s, :, 0:1]
-
-        def columns(j, carry):
-            cols = pl.ds(pl.multiple_of(j * CHUNK, CHUNK), CHUNK)
-            normed_grad = contract_last(pre_b, w[s, cols, :HID])
-            normed = nb[s, :, cols].astype(f32)
-            g[:, cols] = (
-                g[:, cols].astype(f32) + spread * (normed_grad - grad_mean - normed * cross_mean)
+            low = (x[:, cols].astype(f32) + gain * branch).astype(bf16)
+            x[:, cols] = low
+            total = total + folded(low.astype(f32))
+        return total
+
+    lax.fori_loop(0, SECTIONS, forward, total)
+
+    keep = tiled(valid_ref[0, pl.ds(pl.multiple_of(me.c * OWN, OWN), OWN), :]) > 0.5
+    last = SECTIONS - 1
+    gain = tiled(gain_of(last))
+    hidden_grad = jnp.zeros((OWN, HID), f32)
+    for j in range(CHUNKS):
+        cols = cols_of(j)
+        low = jnp.where(keep, x[:, cols].astype(f32), 0.0).astype(bf16)
+        g[:, cols] = low
+        scaled = (gain * low.astype(f32)).astype(bf16)
+        out[last % 2, :, cols] = scaled
+        hidden_grad = hidden_grad + jnp.dot(scaled, w[last, cols, HID:], preferred_element_type=f32)
+
+    @pl.when(sib == last)
+    def _():
+        for p in range(PIECES):
+            send_out(p).start()
+
+    def inner(s, hidden_grad):
+        pre_act = pre[s]
+        scaled = (inv[s] * (gelu_parts(pre_act)[1] * hidden_grad)).astype(bf16)
+        pg[lax.rem(s, 2)] = scaled
+
+        @pl.when(s == sib)
+        def _():
+            send_pg().start()
+
+        return scaled, pre_act
+
+    def backward(i, hidden_grad):
+        s = last - i
+        scaled_pre, pre_act = inner(s, hidden_grad)
+        pre_f = scaled_pre.astype(f32)
+        shift = tiled(row_mean(pre_f * jnp.sum(wsum[s], axis=0, keepdims=True)))
+        slope = tiled(row_mean(pre_f * pre_act) * inv[s])
+        gain = tiled(gain_of(s - 1))
+        slot = lax.rem(s + 1, 2)
+        hidden_grad = jnp.zeros((OWN, HID), f32)
+        for j in range(CHUNKS):
+            cols = cols_of(j)
+            normed_grad = contract_last(scaled_pre, w[s, cols, :HID])
+            low = (
+                g[:, cols].astype(f32) + (normed_grad - shift - cb[s, :, cols].astype(f32) * slope)
             ).astype(bf16)
-            return carry
-
-        lax.fori_loop(0, WIDTH // CHUNK, columns, 0)
-        return carry
-
-    lax.fori_loop(0, SECTIONS - 1 - mine, backward, 0)
-    pre_b = inner_grads(mine)
-    hidden = hid[mine]
-
-    def columns(j, carry):
-        cols = pl.ds(pl.multiple_of(j * CHUNK, CHUNK), CHUNK)
-        grad_ref[cols, :HID] = contract_first(pre_b, nb[mine, :, cols]).T.astype(bf16)
-        grad_ref[cols, HID:] = contract_first(hidden, out_b[:, cols]).T.astype(bf16)
-        return carry
-
-    lax.fori_loop(0, WIDTH // CHUNK, columns, 0)
-
-
-def relay(which, rows, all_weights, gains, valid):
+            g[:, cols] = low
+            scaled = (gain * low.astype(f32)).astype(bf16)
+            out[slot, :, cols] = scaled
+            hidden_grad = hidden_grad + jnp.dot(scaled, w[s - 1, cols, HID:], preferred_element_type=f32)
+            if (j + 1) * CHUNK % PIECE == 0:
+
+                @pl.when(s - 1 == sib)
+                def _():
+                    send_out((j + 1) * CHUNK // PIECE - 1).start()
+
+        return hidden_grad
+
+    hidden_grad = lax.fori_loop(0, last - me.y * 2, backward, hidden_grad)
+    inner(me.y * 2, hidden_grad)
+
+    send_pr().wait()
+    probe_ref[...] = (probe_ref[...].astype(f32) + pr_in[...].astype(f32)).astype(bf16)
+    send_cb().wait()
+    send_hid().wait()
+    send_pg().wait()
+    for p in range(PIECES):
+        send_out(p).wait()
+    pg_a, pg_b, hid_a, hid_b = pg[me.c], pg_in[...], hid[mine], hid_in[...]
+    for j in range(CHUNKS):
+        cols = cols_of(j)
+        first = contract_first(pg_a, cb[mine, :, cols]) + contract_first(pg_b, cb_in[:, cols])
+        grad_ref[cols, :HID] = first.astype(bf16).T
+        second = contract_first(hid_a, out[me.c, :, cols]) + contract_first(hid_b, out_in[:, cols])
+        grad_ref[cols, HID:] = second.astype(bf16).T
+
+
+def relay(rows, all_weights, gains, valid):
     return pl.pallas_call(
         relay_kernel,
         out_shape=(
@@ -409,7 +505,6 @@
             jax.ShapeDtypeStruct((TOK, WIDTH), bf16),
         ),
         in_specs=[
-            pl.BlockSpec(memory_space=pltpu.SMEM),
             pl.BlockSpec(memory_space=pl.ANY),
             pl.BlockSpec(memory_space=pl.ANY),
             pl.BlockSpec(memory_space=pltpu.VMEM),
@@ -421,20 +516,33 @@
         ),
         scratch_shapes=[
             pltpu.VMEM((SECTIONS, WIDTH, 2 * HID), bf16),
-            pltpu.VMEM((ROWS, WIDTH), bf16),
-            pltpu.VMEM((ROWS, WIDTH), bf16),
-            pltpu.VMEM((SECTIONS, ROWS, WIDTH), bf16),
-            pltpu.VMEM((SECTIONS, ROWS, 128), f32),
-            pltpu.VMEM((SECTIONS, ROWS, HID), f32),
-            pltpu.VMEM((SECTIONS, ROWS, HID), bf16),
-            pltpu.VMEM((ROWS, WIDTH), bf16),
-            pltpu.VMEM((SECTIONS, 1, HID), f32),
+            pltpu.VMEM((OWN, WIDTH), bf16),
+            pltpu.VMEM((OWN, WIDTH), bf16),
+            pltpu.VMEM((SECTIONS, OWN, WIDTH), bf16),
+            pltpu.VMEM((SECTIONS, OWN, 128), f32),
+            pltpu.VMEM((SECTIONS, OWN, HID), f32),
+            pltpu.VMEM((SECTIONS, OWN, HID), bf16),
+            pltpu.VMEM((SECTIONS, 8, HID), f32),
+            pltpu.VMEM((2, OWN, WIDTH), bf16),
+            pltpu.VMEM((2, OWN, HID), bf16),
+            pltpu.VMEM((OWN, WIDTH), bf16),
+            pltpu.VMEM((OWN, HID), bf16),
+            pltpu.VMEM((OWN, WIDTH), bf16),
+            pltpu.VMEM((OWN, HID), bf16),
+            pltpu.VMEM((TOK, WIDTH), bf16),
+            pltpu.VMEM((TOK, WIDTH), bf16),
             pltpu.SemaphoreType.DMA((SECTIONS,)),
             pltpu.SemaphoreType.DMA,
+            pltpu.SemaphoreType.DMA((3,)),
+            pltpu.SemaphoreType.DMA((3,)),
+            pltpu.SemaphoreType.DMA((PIECES + 1,)),
+            pltpu.SemaphoreType.DMA((PIECES + 1,)),
         ],
-        compiler_params=pltpu.CompilerParams(vmem_limit_bytes=58 * 2**20),
+        compiler_params=pltpu.CompilerParams(
+            collective_id=2, has_side_effects=True, vmem_limit_bytes=58 * 2**20
+        ),
         name="relay",
-    )(which, rows, all_weights, gains, valid)
+    )(rows, all_weights, gains, valid)
 
 
 HALF = SHARD // 2
@@ -688,13 +796,14 @@
     gain_tile = jnp.full((8, 128), lax.rsqrt(1.0 + layer_index.astype(f32) / 8.0)[0], f32)
     all_weights, gains = gather_all(stashed[0], gain_tile)
     row_pos = lax.broadcasted_iota(jnp.int32, (16, TOK), 1)
-    valid = (row_pos < counts[0][:, None]).astype(f32).reshape(ROWS, 1)
+    valid = row_pos < counts[0][:, None]
+    chosen = lax.broadcasted_iota(jnp.int32, (16, TOK), 0) == plan[15]
+    marks = jnp.stack([valid, chosen]).astype(f32).reshape(2, ROWS, 1)
     grad, probe_in = relay(
-        plan[15:],
         inputs.reshape(ROWS, WIDTH),
         all_weights.reshape(2, NY, WIDTH, 2 * HID),
         gains,
-        jnp.broadcast_to(valid, (ROWS, 128)),
+        jnp.broadcast_to(marks, (2, ROWS, 128)),
     )
     probe_out, new_master, new_first, new_second = finish(
         grad.reshape(NZ, NX, SHARD, 2 * HID), master[0], first_moment[0], second_moment[0], gain_tile, probe_in

time: 333 us -> 243 us (0.73)
  Pallas kernels: 323 us -> 232 us
    pallas_call x1, Pallas kernels: 89.4 us -> 26.5 us  [relay(): pl.pallas_call(relay_kernel, out_shape=(jax.ShapeDtypeStruct((WIDTH, 2 *...]
    pallas_call x1, Pallas kernels: 141 us -> 113 us  [finish(): pl.pallas_call(finish_kernel, out_shape=(jax.ShapeDtypeStruct((TOK, WIDTH...]
where the time goes in v2:
time: 243 us
  Pallas kernels  232 us (95%)
  local copies, waits for them, and re-layouts  8.79 us (4%)
    pallas_call x1, Pallas kernels, finish(): pl.pallas_call(finish_kernel, out_shape=(jax.ShapeDtypeStruct((TOK, WIDTH...  113 us
    pallas_call x1, Pallas kernels, gather_all(): pl.pallas_call(gather_all_kernel, out_shape=(jax.ShapeDtypeStruct((2, NY,...  92.4 us
    pallas_call x1, Pallas kernels, relay(): pl.pallas_call(relay_kernel, out_shape=(jax.ShapeDtypeStruct((WIDTH, 2 *...  26.5 us
    unnamed x16, local copies, waits for them, and re-layouts  5.06 us

profile of v2, /device:TPU:24, one launch (start us, length us, event | category | flops | bytes accessed | tf_op | source)
XLA Modules:
  0.0 242.6 jit_solution(4655697536686263070)
XLA Ops:
  1.3 1.2 slice.3
  2.6 0.6 iota_compare_fusion
  3.2 0.1 stack.9
  3.3 0.1 stack.10
  3.4 0.6 broadcast_in_dim.20.gain_ref
  4.0 0.7 lt.19
  4.7 0.1 lt.20
  4.8 0.1 iota.15
  4.9 0.8 broadcast_in_dim.21.valid_ref
  5.7 92.4 %gather_all.1 = (bf16[2,4,16,4,64,256]{5,4,3,2,1,0:T(8,128)(2,1)}, f32[2,4,8,128]{3,2,1,0:T(8,128)}) custom-call(bf16[64,256]{1,0:T(8,128)(2,1)} %bitcast.26, f32[8,128]{1,0:T(8,128)} %broadcast_in_dim.20.gain_ref), custom_call_target="tpu_custom_call" | custom-call | tf_op jit(solution)/shard_map/gather_all/pallas_call | solution.py:246
  98.1 0.0 copy-start.2
  98.1 0.0 copy-start.3
  98.1 0.0 copy-start.4
  98.1 0.0 copy-start.5
  98.2 26.5 %relay.1 = (bf16[4096,256]{1,0:T(8,128)(2,1)}, bf16[16,4096]{1,0:T(8,128)(2,1)}) custom-call(bf16[256,4096]{1,0:T(8,128)(2,1)} %bitcast.25, bf16[2,4,4096,256]{3,2,1,0:T(8,128)(2,1)} %bitcast.24, f32[2,4,8,128]{3,2,1,0:T(8,128)} %get-tuple-element.13.gains_ref, f32[2,256,128]{2,1,0:T(8,128)} %broadcast_in_dim.21.valid_ref), custom_call_target="tpu_custom_call" | custom-call | tf_op jit(solution)/shard_map/relay/pallas_call | solution.py:501
  124.7 0.0 copy-done.2
  124.7 0.0 copy-done.3
  124.7 0.0 copy-done.4
  124.7 0.0 copy-done.5
  124.7 0.0 copy-start
  124.8 1.6 copy-done
  126.3 0.0 copy-start.1
  126.3 0.9 copy-done.1
  127.2 112.8 %finish.1 = (bf16[16,4096]{1,0:T(8,128)(2,1)S(1)}, f32[64,256]{1,0:T(8,128)S(1)}, f32[64,256]{1,0:T(8,128)S(1)}, f32[64,256]{1,0:T(8,128)S(1)}) custom-call(bf16[16,4,64,256]{3,2,1,0:T(8,128)(2,1)S(1)} %bitcast.16, f32[64,256]{1,0:T(8,128)S(1)} %bitcast.18, f32[64,256]{1,0:T(8,128)S(1)} %bitcast.19, f32[64,256]{1,0:T(8,128)S(1)} %bitcast.20, ...), custom_call_target="tpu_custom_call" | custom-call | tf_op jit(solution)/shard_map/finish/pallas_call | solution.py:762
  240.0 0.7 copy.17
  240.7 0.6 copy.18
  241.3 0.6 copy.19
  241.9 0.6 copy.20
  (3 shorter events, 0.0 us)
Async XLA Ops:
  98.1 26.6 %copy-start.2 = (f32[1,64,256]{2,1,0:T(8,128)S(1)}, f32[1,64,256]{2,1,0:T(8,128)}, u32[]{:S(2)}) copy-start(f32[1,64,256]{2,1,0:T(8,128)} %param.10) | copy-start | bytes 196612
  98.1 26.6 %copy-start.3 = (f32[1,64,256]{2,1,0:T(8,128)S(1)}, f32[1,64,256]{2,1,0:T(8,128)}, u32[]{:S(2)}) copy-start(f32[1,64,256]{2,1,0:T(8,128)} %param.11) | copy-start | bytes 196612
  98.1 26.6 %copy-start.4 = (f32[1,64,256]{2,1,0:T(8,128)S(1)}, f32[1,64,256]{2,1,0:T(8,128)}, u32[]{:S(2)}) copy-start(f32[1,64,256]{2,1,0:T(8,128)} %param.12) | copy-start | bytes 196612
  98.1 26.6 %copy-start.5 = (f32[8,128]{1,0:T(8,128)S(1)}, f32[8,128]{1,0:T(8,128)}, u32[]{:S(2)}) copy-start(f32[8,128]{1,0:T(8,128)} %broadcast_in_dim.20.gain_ref) | copy-start | bytes 12292
  124.7 1.6 copy-start
  126.3 0.9 copy-start.1

commit v3 on v2

v3 whole, which is shorter than its diff:
```python
import functools

import jax
import jax.numpy as jnp
from jax import lax
from jax.experimental import pallas as pl
from jax.experimental.pallas import tpu as pltpu
from jax.sharding import PartitionSpec as P

eps_norm = 1e-05
beta_one = 0.9
beta_two = 0.95
eps_adam = 1e-08
learn_rate = 0.002
decay_rate = 0.1

MESH = pl.DeviceIdType.MESH
WIDTH = 4096
HID = 128
ROWS = 256
TOK = 16
SECTIONS = 8
SHARD = 64
NZ = 16
NX = 4
NY = 4
f32 = jnp.float32
bf16 = jnp.bfloat16


class Place:

    def __init__(self):
        self.s = lax.axis_index("section")
        self.d = lax.axis_index("dp")
        self.c = lax.rem(self.s, 2)
        self.y = self.s // 2
        self.z = self.d // NX
        self.x = lax.rem(self.d, NX)

    def at_z(self, k):
        return (self.s, lax.rem(self.z + k + 2 * NZ, NZ) * NX + self.x)

    def at_x(self, k):
        return (self.s, self.z * NX + lax.rem(self.x + k + NX, NX))

    def at_y(self, k):
        return (lax.rem(self.y + k + NY, NY) * 2 + self.c, self.d)

    def sibling(self):
        return (self.y * 2 + 1 - self.c, self.d)


def greet(partners):
    barrier = pltpu.get_barrier_semaphore()
    for partner in partners:
        pl.semaphore_signal(barrier, inc=1, device_id=partner, device_id_type=MESH)
    pl.semaphore_wait(barrier, len(partners))


def remote(src, dst, send, recv, to):
    return pltpu.make_async_remote_copy(
        src_ref=src, dst_ref=dst, send_sem=send, recv_sem=recv, device_id=to, device_id_type=MESH
    )


def block_z(me, flow, k):
    if flow == 0:
        return lax.rem(me.z - k + 2 * NZ, NZ)
    return lax.rem(me.z + k, NZ)


def last_of(flow):
    return 8 if flow == 0 else 7


def when_in(flow, k, lowest):
    low = max(flow, lowest)
    return pl.when((k >= low) & (k <= last_of(flow)))


class OverX:
    def __init__(self, me, part, at, here, sems):
        self.me, self.part, self.at, self.here = me, part, at, here
        self.ss, self.sr, self.fs, self.fr = sems

    def copy(self, flow, k, side):
        ref = self.part(block_z(self.me, flow, k), self.here)
        to = self.at(1 if side == 0 else -1)
        return remote(ref, ref, self.ss.at[flow, k, side], self.sr.at[flow, k, side], to)

    def onward(self, flow, k):
        came = -1 if flow == 0 else 1
        ref = self.part(block_z(self.me, flow, k), lax.rem(self.here + came + 4, 4))
        return remote(ref, ref, self.fs.at[flow, k], self.fr.at[flow, k], self.at(-came))

    def send(self, flow, k):
        for side in range(2):
            self.copy(flow, k, side).start()

    def pass_on(self, k):
        for flow in range(2):

            @when_in(flow, k, 0)
            def _():
                for side in range(2):
                    self.copy(flow, k, side).wait_recv()
                self.onward(flow, k).start()

    def wait(self, flow, k):
        self.onward(flow, k).wait_recv()

    def drain(self, flow, k):
        for side in range(2):
            self.copy(flow, k, side).wait_send()
        self.onward(flow, k).wait_send()


class RoundZ:
    def __init__(self, me, part, sems, stride):
        self.me, self.part, self.stride = me, part, stride
        self.zs, self.zr = sems[0], sems[1]
        self.over = OverX(me, part, me.at_x, me.x, sems[2:])

    def copy(self, flow, k, hop=1):
        ref = self.part(block_z(self.me, flow, k - hop), self.me.x)
        to = self.me.at_z(hop if flow == 0 else -hop)
        return remote(ref, ref, self.zs.at[flow, k], self.zr.at[flow, k], to)

    def begin(self):
        for hop in range(1, self.stride + 1):
            for flow in range(2):
                self.copy(flow, hop, hop).start()
        self.over.send(0, 0)

    def step(self, j):
        far = j * self.stride
        for flow in range(2):

            @when_in(flow, far, 1)
            def _():
                self.copy(flow, far, self.stride).wait_recv()

                for hop in range(1, self.stride + 1):

                    @pl.when(far + hop <= last_of(flow))
                    def _():
                        self.copy(flow, far + hop, hop).start()

                self.over.send(flow, far)

        if self.stride == 2:
            for flow in range(2):

                @when_in(flow, far - 1, 1)
                def _():
                    self.copy(flow, far - 1, 1).wait_recv()
                    self.over.send(flow, far - 1)

    def steps_of(self, j):
        return [j * self.stride - i for i in range(self.stride)]

    def pass_on(self, j):
        for k in self.steps_of(j):
            self.over.pass_on(k)

    def wait(self, j):
        for k in self.steps_of(j):
            for flow in range(2):

                @when_in(flow, k, 0)
                def _():
                    self.over.wait(flow, k)

    def drain(self, j):
        for i, k in enumerate(self.steps_of(j)):
            for flow in range(2):

                @when_in(flow, k, 1)
                def _():
                    self.copy(flow, k, self.stride - i).wait_send()

                @when_in(flow, k, 0)
                def _():
                    self.over.drain(flow, k)


class BlocksRoundZ:
    def __init__(self, me, part, block, sems, stride):
        self.me, self.part, self.block, self.stride = me, part, block, stride
        self.xs, self.xr, self.zs, self.zr = sems

    def first(self, dx):
        ref = self.part(self.me.z, self.me.x)
        return remote(ref, ref, self.xs.at[dx], self.xr.at[dx], self.me.at_x(dx))

    def copy(self, flow, k, hop, piece):
        ref = self.block(block_z(self.me, flow, k - hop), piece)
        to = self.me.at_z(hop if flow == 0 else -hop)
        return remote(ref, ref, self.zs.at[flow, k, piece], self.zr.at[flow, k, piece], to)

    def begin(self):
        for dx in range(1, NX):
            self.first(dx).start()

    def launch(self):
        for dx in range(1, NX):
            self.first(dx).wait_recv()
        for piece in range(2):
            for hop in range(1, self.stride + 1):
                for flow in range(2):
                    self.copy(flow, hop, hop, piece).start()

    def step(self, j):
        far = j * self.stride
        for piece in range(2):
            for flow in range(2):
                end = 8 if flow == piece else 7

                @pl.when((far >= 1) & (far <= end))
                def _():
                    self.copy(flow, far, self.stride, piece).wait_recv()

                    for hop in range(1, self.stride + 1):

                        @pl.when(far + hop <= end)
                        def _():
                            self.copy(flow, far + hop, hop, piece).start()

        if self.stride == 2:
            for piece in range(2):
                for flow in range(2):

                    @pl.when((far >= 2) & (far <= 8))
                    def _():
                        self.copy(flow, far - 1, 1, piece).wait_recv()

    def drain(self, j):
        for i in range(self.stride):
            k = j * self.stride - i
            for piece in range(2):
                for flow in range(2):

                    @pl.when((k >= 1) & (k <= (8 if flow == piece else 7)))
                    def _():
                        self.copy(flow, k, self.stride - i, piece).wait_send()

    def finish(self):
        for dx in range(1, NX):
            self.first(dx).wait_send()


DMA = pltpu.SemaphoreType.DMA
ROUND_SEMS = [DMA((2, 9)), DMA((2, 9)), DMA((2, 9, 2)), DMA((2, 9, 2)), DMA((2, 9)), DMA((2, 9))]
BLOCK_SEMS = [DMA((NX,)), DMA((NX,)), DMA((2, 9, 2)), DMA((2, 9, 2))]
OVER_SEMS = [DMA((2, 9, 2)), DMA((2, 9, 2)), DMA((2, 9)), DMA((2, 9))]

ROWS_XZ, ROWS_ZX, ROWS_ZXY = 16, 16, 32


def gather_all(me, w_ref, gain_ref, all_ref, gains_ref, ys, yr, gs, gr, ss, sr, own, *sems):
    early = ROWS_XZ + ROWS_ZX

    def ycopy(k):
        rows = pl.ds(0, early)
        dst = all_ref.at[me.c, me.y, me.z, me.x, rows]
        return remote(w_ref.at[rows], dst, ys.at[k], yr.at[k], me.at_y(k))

    def gcopy(k):
        return remote(gain_ref, gains_ref.at[me.c, me.y], gs.at[k], gr.at[k], me.at_y(k))

    keep = pltpu.make_async_copy(w_ref, all_ref.at[me.c, me.y, me.z, me.x], own.at[0])
    keep_gain = pltpu.make_async_copy(gain_ref, gains_ref.at[me.c, me.y], own.at[1])
    keep.start()
    keep_gain.start()
    for k in range(1, NY):
        ycopy(k).start()
        gcopy(k).start()
    keep.wait()

    def late_part(z, x):
        return all_ref.at[me.c, me.y, z, x, pl.ds(early, ROWS_ZXY)]

    def late_column(z, y):
        return all_ref.at[me.c, y, z, :, pl.ds(early, ROWS_ZXY)]

    def mid_part(z, x):
        return all_ref.at[me.c, :, z, x, pl.ds(ROWS_XZ, ROWS_ZX)]

    def early_part(z, x):
        return all_ref.at[me.c, :, z, x, pl.ds(0, ROWS_XZ)]

    def early_block(z, piece):
        return all_ref.at[me.c, pl.ds(2 * piece, 2), z, :, pl.ds(0, ROWS_XZ)]

    late = RoundZ(me, late_part, sems[0:6], 1)
    mid = RoundZ(me, mid_part, sems[6:12], 1)
    blocks = BlocksRoundZ(me, early_part, early_block, sems[12:16], 1)
    over_y = OverX(me, late_column, me.at_y, me.y, sems[16:20])

    def side_copy(flow, k):
        part = all_ref.at[me.c, :, block_z(me, flow, k)]
        return remote(part, part, ss.at[flow, k], sr.at[flow, k], me.sibling())

    late.begin()
    for k in range(1, NY):
        ycopy(k).wait_recv()
    blocks.begin()
    mid.begin()
    keep_gain.wait()
    for k in range(1, NY):
        gcopy(k).wait_recv()
    gains = remote(gains_ref.at[me.c], gains_ref.at[me.c], ss.at[2, 0], sr.at[2, 0], me.sibling())
    gains.start()

    def drain(k):
        late.drain(k)
        mid.drain(k)
        blocks.drain(k)
        for flow in range(2):

            @when_in(flow, k, 0)
            def _():
                over_y.drain(flow, k)

    def step(t, carry):
        late.step(t)
        mid.step(t - 1)
        late.pass_on(t - 1)
        mid.pass_on(t - 2)
        late.wait(t - 2)
        for flow in range(2):

            @when_in(flow, t - 2, 0)
            def _():
                over_y.send(flow, t - 2)

        mid.wait(t - 3)
        over_y.pass_on(t - 3)

        @pl.when(t == 2)
        def _():
            blocks.launch()

        blocks.step(t - 2)
        for flow in range(2):

            @when_in(flow, t - 4, 0)
            def _():
                over_y.wait(flow, t - 4)
                side_copy(flow, t - 4).start()

        drain(t - 6)
        return carry

    lax.fori_loop(1, 13, step, 0)

    for k in (7, 8):
        drain(k)
    blocks.finish()

    def finish(k, carry):
        for flow in range(2):

            @when_in(flow, k, 0)
            def _():
                side_copy(flow, k).wait()

        return carry

    lax.fori_loop(0, 9, finish, 0)
    gains.wait()
    for k in range(1, NY):
        ycopy(k).wait_send()
        gcopy(k).wait_send()


def normalize(values):
    centred = values - jnp.mean(values, axis=-1, keepdims=True)
    inv_spread = lax.rsqrt(jnp.mean(centred * centred, axis=-1, keepdims=True) + eps_norm)
    return (centred * inv_spread, inv_spread)


def contract_last(lhs_array, rhs_array):
    return lax.dot_general(
        lhs_array, rhs_array, (((1,), (1,)), ((), ())), preferred_element_type=f32
    )


def contract_first(lhs_array, rhs_array):
    return lax.dot_general(
        lhs_array, rhs_array, (((0,), (0,)), ((), ())), preferred_element_type=f32
    )


root_two_over_pi = 0.7978845608028654
cubic = 0.044715


def gelu_parts(v):
    t = jnp.tanh(root_two_over_pi * (v + cubic * (v * v * v)))
    cdf = 0.5 * (1.0 + t)
    slope = cdf + 0.5 * v * (1.0 - t * t) * (root_two_over_pi * (1.0 + 3.0 * cubic * v * v))
    return v * cdf, slope


OWN = ROWS // 2
CHUNK = 512
CHUNKS = WIDTH // CHUNK
PIECES = 4
PIECE = WIDTH // PIECES


def tiled(a):
    return jnp.concatenate([a] * (CHUNK // 128), axis=1)


def folded(a):
    total = a[:, 0:128]
    for i in range(1, a.shape[1] // 128):
        total = total + a[:, i * 128 : (i + 1) * 128]
    return total


def row_mean(a):
    return jnp.broadcast_to(jnp.sum(a, axis=-1, keepdims=True) * (1.0 / WIDTH), (OWN, 128))


def relay(
    me, w, gains_ref, valid_ref, grad_ref, probe_ref,
    x, g, cb, inv, pre, hid, wsum, out, pg, cb_in, hid_in, out_in, pg_in, pr, pr_in,
    fs, fr, bs, br,
):
    mine = me.s
    sib = me.y * 2 + 1 - me.c

    def span(j):
        return slice(j * (CHUNK // 256), (j + 1) * (CHUNK // 256))

    def weight(s, j, half):
        cols = slice(half * HID, (half + 1) * HID)
        return w[lax.rem(s, 2), s // 2, span(j), :, :, cols].reshape(CHUNK, HID)

    def send_cb():
        return remote(cb.at[sib], cb_in, fs.at[0], fr.at[0], me.sibling())

    def send_hid():
        return remote(hid.at[sib], hid_in, fs.at[1], fr.at[1], me.sibling())

    def send_pr():
        return remote(pr, pr_in, fs.at[2], fr.at[2], me.sibling())

    def send_out(p):
        cols = pl.ds(p * PIECE, PIECE)
        return remote(out.at[1 - me.c, :, cols], out_in.at[:, cols], bs.at[p], br.at[p], me.sibling())

    def send_pg():
        return remote(pg.at[1 - me.c], pg_in, bs.at[PIECES], br.at[PIECES], me.sibling())

    def gain_of(s):
        return gains_ref[lax.rem(s, 2), s // 2, 0:1, :]

    def cols_of(j):
        return slice(j * CHUNK, (j + 1) * CHUNK)

    def picked(ref):
        for j in range(CHUNKS):
            cols = cols_of(j)
            rows = jnp.zeros((TOK, CHUNK), f32)
            for i in range(OWN // TOK):
                part = pl.ds(i * TOK, TOK)
                chosen = valid_ref[1, pl.ds(pl.multiple_of(me.c * OWN + i * TOK, TOK), TOK), :]
                rows = rows + tiled(chosen) * x[part, cols].astype(f32)
            ref[:, cols] = rows.astype(bf16)

    total = jnp.zeros((OWN, 128), f32)
    for j in range(CHUNKS):
        total = total + folded(x[:, cols_of(j)].astype(f32))

    def forward(s, total):
        @pl.when(s == mine)
        def _():
            picked(probe_ref)

        @pl.when(s == sib)
        def _():
            picked(pr)
            send_pr().start()

        mean = tiled(row_mean(total))
        squares = jnp.zeros((OWN, 128), f32)
        acc = jnp.zeros((OWN, HID), f32)
        columns = jnp.zeros((8, 128), f32)
        for j in range(CHUNKS):
            cols = cols_of(j)
            centred = x[:, cols].astype(f32) - mean
            squares = squares + folded(centred * centred)
            low = centred.astype(bf16)
            cb[s, :, cols] = low
            part = weight(s, j, 0)
            acc = acc + jnp.dot(low, part, preferred_element_type=f32)
            columns = columns + jnp.sum(part.astype(f32).reshape(CHUNK // 8, 8, HID), axis=0)
        wsum[s] = columns
        spread = lax.rsqrt(row_mean(squares) + eps_norm)
        inv[s] = spread
        pre_act = acc * spread
        pre[s] = pre_act
        hidden = gelu_parts(pre_act)[0].astype(bf16)
        hid[s] = hidden

        @pl.when(s == sib)
        def _():
            send_cb().start()
            send_hid().start()

        gain = tiled(gain_of(s))
        total = jnp.zeros((OWN, 128), f32)
        for j in range(CHUNKS):
            cols = cols_of(j)
            branch = contract_last(hidden, weight(s, j, 1))
            low = (x[:, cols].astype(f32) + gain * branch).astype(bf16)
            x[:, cols] = low
            total = total + folded(low.astype(f32))
        return total

    lax.fori_loop(0, SECTIONS, forward, total)

    keep = tiled(valid_ref[0, pl.ds(pl.multiple_of(me.c * OWN, OWN), OWN), :]) > 0.5
    last = SECTIONS - 1
    gain = tiled(gain_of(last))
    hidden_grad = jnp.zeros((OWN, HID), f32)
    for j in range(CHUNKS):
        cols = cols_of(j)
        low = jnp.where(keep, x[:, cols].astype(f32), 0.0).astype(bf16)
        g[:, cols] = low
        scaled = (gain * low.astype(f32)).astype(bf16)
        out[1, :, cols] = scaled
        hidden_grad = hidden_grad + jnp.dot(scaled, weight(last, j, 1), preferred_element_type=f32)

    @pl.when(sib == last)
    def _():
        for p in range(PIECES):
            send_out(p).start()

    def inner(s, hidden_grad):
        pre_act = pre[s]
        scaled = (inv[s] * (gelu_parts(pre_act)[1] * hidden_grad)).astype(bf16)
        pg[lax.rem(s, 2)] = scaled

        @pl.when(s == sib)
        def _():
            send_pg().start()

        return scaled, pre_act

    def backward(i, hidden_grad):
        s = last - i
        scaled_pre, pre_act = inner(s, hidden_grad)
        pre_f = scaled_pre.astype(f32)
        shift = tiled(row_mean(pre_f * jnp.sum(wsum[s], axis=0, keepdims=True)))
        slope = tiled(row_mean(pre_f * pre_act) * inv[s])
        gain = tiled(gain_of(s - 1))
        slot = lax.rem(s + 1, 2)
        hidden_grad = jnp.zeros((OWN, HID), f32)
        for j in range(CHUNKS):
            cols = cols_of(j)
            normed_grad = contract_last(scaled_pre, weight(s, j, 0))
            low = (
                g[:, cols].astype(f32) + (normed_grad - shift - cb[s, :, cols].astype(f32) * slope)
            ).astype(bf16)
            g[:, cols] = low
            scaled = (gain * low.astype(f32)).astype(bf16)
            out[slot, :, cols] = scaled
            hidden_grad = hidden_grad + jnp.dot(scaled, weight(s - 1, j, 1), preferred_element_type=f32)
            if (j + 1) * CHUNK % PIECE == 0:

                @pl.when(s - 1 == sib)
                def _():
                    send_out((j + 1) * CHUNK // PIECE - 1).start()

        return hidden_grad

    hidden_grad = lax.fori_loop(0, last - me.y * 2, backward, hidden_grad)
    inner(me.y * 2, hidden_grad)

    send_pr().wait()
    probe_ref[...] = (probe_ref[...].astype(f32) + pr_in[...].astype(f32)).astype(bf16)
    send_cb().wait()
    send_hid().wait()
    send_pg().wait()
    for p in range(PIECES):
        send_out(p).wait()
    pg_a, pg_b, hid_a, hid_b = pg[me.c], pg_in[...], hid[mine], hid_in[...]
    for j in range(CHUNKS):
        cols = cols_of(j)
        first = contract_first(pg_a, cb[mine, :, cols]) + contract_first(pg_b, cb_in[:, cols])
        grad_ref[span(j), :, :, :HID] = first.astype(bf16).T.reshape(CHUNK // 256, NX, SHARD, HID)
        second = contract_first(hid_a, out[me.c, :, cols]) + contract_first(hid_b, out_in[:, cols])
        grad_ref[span(j), :, :, HID:] = second.astype(bf16).T.reshape(CHUNK // 256, NX, SHARD, HID)


ROWS_Z, ROWS_X = 32, 32
FRESH_XZ, FRESH_ZX = 16, 48
GROUP = SECTIONS * NX


class SumRoundZ:
    def __init__(self, me, own, held, sems, index):
        self.me, self.own, self.held, self.index = me, own, held, index
        self.zs, self.zr = sems

    def target(self, flow, k):
        return block_z(self.me, 1 - flow, k)

    def copy(self, flow, k):
        first = k % 2 == 1 or k == 8
        hop = 1 if k % 2 else 2
        to = self.me.at_z(hop if flow == 0 else -hop)
        src = self.own(self.target(flow, k)) if first else self.held(flow, k + 2 if k < 6 or flow == 0 else 7)
        return remote(src, self.held(flow, k), self.zs.at[flow, k, self.index], self.zr.at[flow, k, self.index], to)

    def begin(self):
        for k in (8, 7, 5, 3, 1):
            for flow in range(2):
                if k <= last_of(flow):
                    self.copy(flow, k).start()

    def step(self, k):
        for flow in range(2):
            into = k + 2 if k < 6 or flow == 0 else 7
            for i in ((7, 8) if k == 6 else (k + 1, k + 2)):
                if i <= last_of(flow):
                    self.copy(flow, i).wait_recv()
            own = self.own(self.target(flow, k))
            total = own[...].astype(f32) + self.held(flow, into)[...].astype(f32)
            if into != k + 1:
                total = total + self.held(flow, k + 1)[...].astype(f32)
            self.held(flow, into)[...] = total.astype(bf16)
            self.copy(flow, k).start()

    def wait(self):
        for flow in range(2):
            for k in (1, 2):
                self.copy(flow, k).wait_recv()

    def result(self):
        total = self.own(self.me.z)[...].astype(f32)
        for flow in range(2):
            for k in (1, 2):
                total = total + self.held(flow, k)[...].astype(f32)
        return total

    def drain(self):
        for flow in range(2):
            for k in range(1, last_of(flow) + 1):
                self.copy(flow, k).wait_send()


def finish(
    me, grad_ref, master_ref, first_ref, second_ref, gain_ref, probe_ref,
    out_ref, new_master_ref, new_first_ref, new_second_ref,
    fresh, ra, rb, xa, xa_out, xb, tb, share, near, far,
    zs, zr, xs, xr, ns, nr, ms, mr, *sems,
):
    def group_at(i):
        ds, dx = i // NX, lax.rem(i, NX)
        return (lax.rem(me.s + ds, SECTIONS), me.z * NX + lax.rem(me.x + dx, NX))

    def xbcopy(dx):
        src = grad_ref.at[:, lax.rem(me.x + dx, NX), pl.ds(ROWS_Z, ROWS_X), :]
        return remote(src, xb.at[dx], xs.at[1, dx], xr.at[1, dx], me.at_x(dx))

    def xacopy(dx):
        src = xa_out.at[lax.rem(me.x + dx, NX)]
        return remote(src, xa.at[dx], xs.at[0, dx], xr.at[0, dx], me.at_x(dx))

    def piece_sum(piece):
        pair = pl.ds(2 * piece, 2)
        return SumRoundZ(
            me,
            lambda z: grad_ref.at[z, pair, pl.ds(0, ROWS_Z), :],
            lambda flow, k: ra.at[flow, k, pair],
            (zs, zr),
            piece,
        )

    pieces = [piece_sum(0), piece_sum(1)]
    late = SumRoundZ(me, lambda z: tb.at[z], lambda flow, k: rb.at[flow, k], (zs, zr), 2)
    for piece in pieces:
        piece.begin()
    for dx in range(1, NX):
        xbcopy(dx).start()
    for piece in pieces:
        piece.step(6)
    for piece in pieces:
        piece.step(4)
    for dx in range(1, NX):
        xbcopy(dx).wait_recv()

    def add(z, carry):
        total = grad_ref[z, me.x, pl.ds(ROWS_Z, ROWS_X), :].astype(f32)
        for dx in range(1, NX):
            total = total + xb[dx, z].astype(f32)
        tb[z] = total.astype(bf16)
        return carry

    lax.fori_loop(0, NZ, add, 0)
    late.begin()
    for piece in pieces:
        piece.step(2)
    late.step(6)
    for i, piece in enumerate(pieces):
        piece.wait()
        xa_out[pl.ds(2 * i, 2)] = piece.result().astype(bf16)
    for dx in range(1, NX):
        xacopy(dx).start()
    late.step(4)
    late.step(2)
    for dx in range(1, NX):
        xacopy(dx).wait_recv()
    total = xa_out[me.x].astype(f32)
    for dx in range(1, NX):
        total = total + xa[dx].astype(f32)
    share[pl.ds(0, ROWS_Z), :] = total
    late.wait()
    share[pl.ds(ROWS_Z, ROWS_X), :] = late.result()

    squares = jnp.zeros((8, 128), f32)
    for i in range(SHARD // 8):
        for j in range(2):
            tile = share[pl.ds(i * 8, 8), pl.ds(j * 128, 128)]
            squares = squares + tile * tile
    near[0] = squares

    def ncopy(i):
        return remote(near.at[0], near.at[i], ns.at[i], nr.at[i], group_at(i))

    def mcopy(k):
        return remote(far.at[0], far.at[k], ms.at[k], mr.at[k], me.at_z(k))

    def n_start(i, carry):
        ncopy(i).start()
        return carry

    def n_wait(i, carry):
        ncopy(i).wait()
        return carry

    def m_start(i, carry):
        mcopy(i).start()
        return carry

    def m_wait(i, carry):
        mcopy(i).wait()
        return carry

    lax.fori_loop(1, GROUP, n_start, 0)
    lax.fori_loop(1, GROUP, n_wait, 0)
    far[0] = jnp.sum(near[...], axis=0)
    lax.fori_loop(1, NZ, m_start, 0)
    lax.fori_loop(1, NZ, m_wait, 0)
    norm_sq = jnp.sum(jnp.sum(far[...], axis=0), keepdims=True)

    clip_factor = 1.0 / jnp.maximum(jnp.sqrt(norm_sq), 1.0)
    clipped = share[...] * clip_factor
    master_now = master_ref[...]
    new_first = beta_one * first_ref[...] + (1.0 - beta_one) * clipped
    new_second = beta_two * second_ref[...] + (1.0 - beta_two) * clipped * clipped
    new_master = master_now - learn_rate * (
        new_first / (jnp.sqrt(new_second) + eps_adam) + decay_rate * master_now
    )
    fresh[me.z, me.x] = new_master.astype(bf16)
    new_master_ref[...] = new_master
    new_first_ref[...] = new_first
    new_second_ref[...] = new_second

    def early_part(z, x):
        return fresh.at[z, x, pl.ds(0, FRESH_XZ)]

    def early_block(z, piece):
        return fresh.at[z, pl.ds(2 * piece, 2), pl.ds(0, FRESH_XZ)]

    def mid_part(z, x):
        return fresh.at[z, x, pl.ds(FRESH_XZ, FRESH_ZX)]

    mid = RoundZ(me, mid_part, sems[0:6], 2)
    blocks = BlocksRoundZ(me, early_part, early_block, sems[6:10], 2)
    blocks.begin()
    mid.begin()
    blocks.launch()

    def step(t, carry):
        mid.step(t)
        blocks.step(t)
        mid.pass_on(t - 1)
        mid.wait(t - 2)
        return carry

    lax.fori_loop(1, 7, step, 0)
    values = probe_ref[...].astype(f32)
    normed = normalize(values)[0].astype(bf16)
    pre_act = jnp.zeros((TOK, HID), f32)
    for z in range(NZ):
        part = fresh[z, :, :, :HID].reshape(256, HID)
        pre_act = pre_act + jnp.dot(normed[:, z * 256 : (z + 1) * 256], part, preferred_element_type=f32)
    hidden = gelu_parts(pre_act)[0].astype(bf16)
    gain = gain_ref[0:1, 0:1]
    for z in range(NZ):
        part = fresh[z, :, :, HID:].reshape(256, HID)
        cols = slice(z * 256, (z + 1) * 256)
        out_ref[:, cols] = (values[:, cols] + gain * contract_last(hidden, part)).astype(bf16)
    def drain(t, carry):
        mid.drain(t)
        blocks.drain(t)
        return carry

    lax.fori_loop(0, 5, drain, 0)
    blocks.finish()
    for piece in pieces:
        piece.drain()
    late.drain()
    for dx in range(1, NX):
        xbcopy(dx).wait_send()
        xacopy(dx).wait_send()


def partners(me):
    ys = [me.at_y(k) for k in range(1, NY)]
    xs = [me.at_x(k) for k in range(1, NX)]
    return ys + xs + [me.at_z(k) for k in (1, 2, -1, -2)] + [me.sibling()]


N_GATHER, N_RELAY, N_FINISH = 27, 4, 18


def step_kernel(
    w_ref, gain_ref, x_hbm, marks_ref, master_ref, first_ref, second_ref,
    out_ref, new_master_ref, new_first_ref, new_second_ref,
    w, gains, grad, probe,
    x, g, cb, inv, pre, hid, wsum, out, pg, cb_in, hid_in, out_in, pg_in, pr, pr_in,
    fresh, ra, rb, xa, xa_out, xb, tb, share, near, far,
    x_sem, *sems,
):
    me = Place()
    get_x = pltpu.make_async_copy(
        x_hbm.at[pl.ds(pl.multiple_of(me.c * OWN, OWN), OWN)], x, x_sem
    )
    get_x.start()
    greet(partners(me))
    gather_all(me, w_ref, gain_ref, w, gains, *sems[:N_GATHER])
    get_x.wait()
    relay(
        me, w, gains, marks_ref, grad, probe,
        x, g, cb, inv, pre, hid, wsum, out, pg, cb_in, hid_in, out_in, pg_in, pr, pr_in,
        *sems[N_GATHER : N_GATHER + N_RELAY],
    )
    finish(
        me, grad, master_ref, first_ref, second_ref, gain_ref, probe,
        out_ref, new_master_ref, new_first_ref, new_second_ref,
        fresh, ra, rb, xa, xa_out, xb, tb, share, near, far,
        *sems[N_GATHER + N_RELAY :],
    )


def shards(inputs, stashed, master, first_moment, second_moment, counts, plan, layer_index):
    gain_tile = jnp.full((8, 128), lax.rsqrt(1.0 + layer_index.astype(f32) / 8.0)[0], f32)
    row_pos = lax.broadcasted_iota(jnp.int32, (16, TOK), 1)
    valid = row_pos < counts[0][:, None]
    chosen = lax.broadcasted_iota(jnp.int32, (16, TOK), 0) == plan[15]
    marks = jnp.stack([valid, chosen]).astype(f32).reshape(2, ROWS, 1)
    state = jax.ShapeDtypeStruct((SHARD, 2 * HID), f32)
    vmem = pl.BlockSpec(memory_space=pltpu.VMEM)
    chunks = (NZ, NX, SHARD, 2 * HID)
    probe_out, new_master, new_first, new_second = pl.pallas_call(
        step_kernel,
        out_shape=(jax.ShapeDtypeStruct((TOK, WIDTH), bf16), state, state, state),
        in_specs=[vmem, vmem, pl.BlockSpec(memory_space=pl.ANY), vmem, vmem, vmem, vmem],
        out_specs=(vmem,) * 4,
        scratch_shapes=[
            pltpu.VMEM((2, NY, *chunks), bf16),
            pltpu.VMEM((2, NY, 8, 128), f32),
            pltpu.VMEM(chunks, bf16),
            pltpu.VMEM((TOK, WIDTH), bf16),
            pltpu.VMEM((OWN, WIDTH), bf16),
            pltpu.VMEM((OWN, WIDTH), bf16),
            pltpu.VMEM((SECTIONS, OWN, WIDTH), bf16),
            pltpu.VMEM((SECTIONS, OWN, 128), f32),
            pltpu.VMEM((SECTIONS, OWN, HID), f32),
            pltpu.VMEM((SECTIONS, OWN, HID), bf16),
            pltpu.VMEM((SECTIONS, 8, HID), f32),
            pltpu.VMEM((2, OWN, WIDTH), bf16),
            pltpu.VMEM((2, OWN, HID), bf16),
            pltpu.VMEM((OWN, WIDTH), bf16),
            pltpu.VMEM((OWN, HID), bf16),
            pltpu.VMEM((OWN, WIDTH), bf16),
            pltpu.VMEM((OWN, HID), bf16),
            pltpu.VMEM((TOK, WIDTH), bf16),
            pltpu.VMEM((TOK, WIDTH), bf16),
            pltpu.VMEM(chunks, bf16),
            pltpu.VMEM((2, 9, NX, ROWS_Z, 2 * HID), bf16),
            pltpu.VMEM((2, 9, ROWS_X, 2 * HID), bf16),
            pltpu.VMEM((NX, ROWS_Z, 2 * HID), bf16),
            pltpu.VMEM((NX, ROWS_Z, 2 * HID), bf16),
            pltpu.VMEM((NX, NZ, ROWS_X, 2 * HID), bf16),
            pltpu.VMEM((NZ, ROWS_X, 2 * HID), bf16),
            pltpu.VMEM((SHARD, 2 * HID), f32),
            pltpu.VMEM((GROUP, 8, 128), f32),
            pltpu.VMEM((NZ, 8, 128), f32),
            DMA,
            *[DMA((NY,))] * 4,
            *[DMA((3, 9))] * 2,
            DMA((2,)),
            *ROUND_SEMS,
            *ROUND_SEMS,
            *BLOCK_SEMS,
            *OVER_SEMS,
            *[DMA((3,))] * 2,
            *[DMA((PIECES + 1,))] * 2,
            *[DMA((2, 9, 3))] * 2,
            *[DMA((2, NX))] * 2,
            *[DMA((GROUP,))] * 2,
            *[DMA((NZ,))] * 2,
            *ROUND_SEMS,
            *BLOCK_SEMS,
        ],
        compiler_params=pltpu.CompilerParams(
            collective_id=0, has_side_effects=True, vmem_limit_bytes=60 * 2**20
        ),
        name="optimizer_step",
    )(
        stashed[0], gain_tile, inputs.reshape(ROWS, WIDTH),
        jnp.broadcast_to(marks, (2, ROWS, 128)), master[0], first_moment[0], second_moment[0],
    )
    return (probe_out[None], new_master[None], new_first[None], new_second[None])


def solution(mesh):
    in_specs = (
        P(None, "dp", None),
        P("section", "dp", None),
        P("section", "dp", None),
        P("section", "dp", None),
        P("section", "dp", None),
        P("dp", None),
        P(),
        P("section"),
    )
    out_specs = (
        P("section", "dp", None),
        P("section", "dp", None),
        P("section", "dp", None),
        P("section", "dp", None),
    )
    return jax.shard_map(shards, mesh=mesh, in_specs=in_specs, out_specs=out_specs, check_vma=False)
```

time: 243 us -> 189 us (0.78)
  Pallas kernels: 232 us -> 176 us
    pallas_call x3 -> x1, Pallas kernels: 232 us -> 176 us  [shards(): pl.pallas_call(step_kernel, out_shape=(jax.ShapeDtypeStruct((TOK, WIDTH),...]
    unnamed x16 -> x4, local copies, waits for them, and re-layouts: 5.06 us -> 5.98 us
where the time goes in v3:
time: 189 us; the launch traced here: 188 us
  Pallas kernels  176 us (93%)
  local copies, waits for them, and re-layouts  9.71 us (5%)
    pallas_call x1, Pallas kernels, shards(): pl.pallas_call(step_kernel, out_shape=(jax.ShapeDtypeStruct((TOK, WIDTH),...  176 us
    unnamed x4, local copies, waits for them, and re-layouts  5.98 us

profile of v3, /device:TPU:24, one launch (start us, length us, event | category | flops | bytes accessed | tf_op | source)
XLA Modules:
  0.0 188.2 jit_solution(9139882146129511487)
XLA Ops:
  1.3 1.2 slice.3
  2.6 0.6 iota_compare_fusion
  3.2 0.1 stack.9
  3.3 0.1 stack.10
  3.4 0.6 broadcast_in_dim.20.gain_ref
  4.0 0.7 lt.19
  4.7 0.1 lt.20
  4.8 0.1 iota.15
  4.9 0.8 broadcast_in_dim.21.marks_ref
  5.7 176.5 %optimizer_step.1 = (bf16[16,4096]{1,0:T(8,128)(2,1)}, f32[64,256]{1,0:T(8,128)}, f32[64,256]{1,0:T(8,128)}, f32[64,256]{1,0:T(8,128)}) custom-call(bf16[64,256]{1,0:T(8,128)(2,1)} %bitcast.22, f32[8,128]{1,0:T(8,128)} %broadcast_in_dim.20.gain_ref, bf16[256,4096]{1,0:T(8,128)(2,1)} %bitcast.14, f32[2,256,128]{2,1,0:T(8,128)} %broadcast_in_dim.21.marks_ref, ...), custom_call_target="tpu_custom_call" | custom-call | tf_op jit(solution)/shard_map/optimizer_step/pallas_call | solution.py:874
  182.2 1.6 copy.17
  183.8 1.5 copy.18
  185.2 1.5 copy.19
  186.7 1.5 copy.20
  (3 shorter events, 0.0 us)

commit v4 on v3

--- a/solution.py
+++ b/solution.py
@@ -74,9 +74,8 @@
     return 8 if flow == 0 else 7
 
 
-def when_in(flow, k, lowest):
-    low = max(flow, lowest)
-    return pl.when((k >= low) & (k <= last_of(flow)))
+def inside(flow, k, lowest):
+    return max(flow, lowest) <= k <= last_of(flow)
 
 
 class OverX:
@@ -100,9 +99,7 @@
 
     def pass_on(self, k):
         for flow in range(2):
-
-            @when_in(flow, k, 0)
-            def _():
+            if inside(flow, k, 0):
                 for side in range(2):
                     self.copy(flow, k, side).wait_recv()
                 self.onward(flow, k).start()
@@ -136,24 +133,18 @@
     def step(self, j):
         far = j * self.stride
         for flow in range(2):
-
-            @when_in(flow, far, 1)
-            def _():
+            if inside(flow, far, 1):
                 self.copy(flow, far, self.stride).wait_recv()
 
                 for hop in range(1, self.stride + 1):
-
-                    @pl.when(far + hop <= last_of(flow))
-                    def _():
+                    if far + hop <= last_of(flow):
                         self.copy(flow, far + hop, hop).start()
 
                 self.over.send(flow, far)
 
         if self.stride == 2:
             for flow in range(2):
-
-                @when_in(flow, far - 1, 1)
-                def _():
+                if inside(flow, far - 1, 1):
                     self.copy(flow, far - 1, 1).wait_recv()
                     self.over.send(flow, far - 1)
 
@@ -167,21 +158,15 @@
     def wait(self, j):
         for k in self.steps_of(j):
             for flow in range(2):
-
-                @when_in(flow, k, 0)
-                def _():
+                if inside(flow, k, 0):
                     self.over.wait(flow, k)
 
     def drain(self, j):
         for i, k in enumerate(self.steps_of(j)):
             for flow in range(2):
-
-                @when_in(flow, k, 1)
-                def _():
+                if inside(flow, k, 1):
                     self.copy(flow, k, self.stride - i).wait_send()
-
-                @when_in(flow, k, 0)
-                def _():
+                if inside(flow, k, 0):
                     self.over.drain(flow, k)
 
 
@@ -216,23 +201,17 @@
         for piece in range(2):
             for flow in range(2):
                 end = 8 if flow == piece else 7
-
-                @pl.when((far >= 1) & (far <= end))
-                def _():
+                if 1 <= far <= end:
                     self.copy(flow, far, self.stride, piece).wait_recv()
 
                     for hop in range(1, self.stride + 1):
-
-                        @pl.when(far + hop <= end)
-                        def _():
+                        if far + hop <= end:
                             self.copy(flow, far + hop, hop, piece).start()
 
         if self.stride == 2:
             for piece in range(2):
                 for flow in range(2):
-
-                    @pl.when((far >= 2) & (far <= 8))
-                    def _():
+                    if 2 <= far <= 8:
                         self.copy(flow, far - 1, 1, piece).wait_recv()
 
     def drain(self, j):
@@ -240,9 +219,7 @@
             k = j * self.stride - i
             for piece in range(2):
                 for flow in range(2):
-
-                    @pl.when((k >= 1) & (k <= (8 if flow == piece else 7)))
-                    def _():
+                    if 1 <= k <= (8 if flow == piece else 7):
                         self.copy(flow, k, self.stride - i, piece).wait_send()
 
     def finish(self):
@@ -258,7 +235,7 @@
 ROWS_XZ, ROWS_ZX, ROWS_ZXY = 16, 16, 32
 
 
-def gather_all(me, w_ref, gain_ref, all_ref, gains_ref, ys, yr, gs, gr, ss, sr, own, *sems):
+def gather_all(me, w_ref, keep, ready, all_ref, gains_ref, gain_ref, ys, yr, gs, gr, ss, sr, *sems):
     early = ROWS_XZ + ROWS_ZX
 
     def ycopy(k):
@@ -267,15 +244,11 @@
         return remote(w_ref.at[rows], dst, ys.at[k], yr.at[k], me.at_y(k))
 
     def gcopy(k):
-        return remote(gain_ref, gains_ref.at[me.c, me.y], gs.at[k], gr.at[k], me.at_y(k))
-
-    keep = pltpu.make_async_copy(w_ref, all_ref.at[me.c, me.y, me.z, me.x], own.at[0])
-    keep_gain = pltpu.make_async_copy(gain_ref, gains_ref.at[me.c, me.y], own.at[1])
-    keep.start()
-    keep_gain.start()
+        part = gains_ref.at[me.c, me.y]
+        return remote(part, part, gs.at[k], gr.at[k], me.at_y(k))
+
     for k in range(1, NY):
         ycopy(k).start()
-        gcopy(k).start()
     keep.wait()
 
     def late_part(z, x):
@@ -293,7 +266,7 @@
     def early_block(z, piece):
         return all_ref.at[me.c, pl.ds(2 * piece, 2), z, :, pl.ds(0, ROWS_XZ)]
 
-    late = RoundZ(me, late_part, sems[0:6], 1)
+    late = RoundZ(me, late_part, sems[0:6], 2)
     mid = RoundZ(me, mid_part, sems[6:12], 1)
     blocks = BlocksRoundZ(me, early_part, early_block, sems[12:16], 1)
     over_y = OverX(me, late_column, me.at_y, me.y, sems[16:20])
@@ -301,78 +274,73 @@
     def side_copy(flow, k):
         part = all_ref.at[me.c, :, block_z(me, flow, k)]
         return remote(part, part, ss.at[flow, k], sr.at[flow, k], me.sibling())
+
+    def both(k):
+        return [flow for flow in range(2) if inside(flow, k, 0)]
 
     late.begin()
     for k in range(1, NY):
         ycopy(k).wait_recv()
     blocks.begin()
     mid.begin()
-    keep_gain.wait()
+    ready()
+    gains_ref[me.c, me.y] = gain_ref[...]
     for k in range(1, NY):
-        gcopy(k).wait_recv()
+        gcopy(k).start()
     gains = remote(gains_ref.at[me.c], gains_ref.at[me.c], ss.at[2, 0], sr.at[2, 0], me.sibling())
-    gains.start()
 
     def drain(k):
-        late.drain(k)
         mid.drain(k)
         blocks.drain(k)
-        for flow in range(2):
-
-            @when_in(flow, k, 0)
-            def _():
-                over_y.drain(flow, k)
-
-    def step(t, carry):
+        for flow in both(k):
+            over_y.drain(flow, k)
+
+    passed = [max(0, min(9, (t - 2) * 9 // 7)) for t in range(12)]
+    for t in range(1, 11):
         late.step(t)
-        mid.step(t - 1)
+        mid.step(t)
         late.pass_on(t - 1)
-        mid.pass_on(t - 2)
+        mid.pass_on(t - 1)
         late.wait(t - 2)
-        for flow in range(2):
-
-            @when_in(flow, t - 2, 0)
-            def _():
-                over_y.send(flow, t - 2)
-
-        mid.wait(t - 3)
-        over_y.pass_on(t - 3)
-
-        @pl.when(t == 2)
-        def _():
+        for k in late.steps_of(t - 2):
+            for flow in both(k):
+                over_y.send(flow, k)
+        for k in range(passed[t - 1], passed[t]):
+            over_y.pass_on(k)
+        blocks.step(t - 1)
+        if t == 1:
             blocks.launch()
-
-        blocks.step(t - 2)
-        for flow in range(2):
-
-            @when_in(flow, t - 4, 0)
-            def _():
-                over_y.wait(flow, t - 4)
-                side_copy(flow, t - 4).start()
-
-        drain(t - 6)
-        return carry
-
-    lax.fori_loop(1, 13, step, 0)
-
-    for k in (7, 8):
-        drain(k)
-    blocks.finish()
-
-    def finish(k, carry):
-        for flow in range(2):
-
-            @when_in(flow, k, 0)
-            def _():
-                side_copy(flow, k).wait()
-
-        return carry
-
-    lax.fori_loop(0, 9, finish, 0)
-    gains.wait()
-    for k in range(1, NY):
-        ycopy(k).wait_send()
-        gcopy(k).wait_send()
+        if t == 4:
+            for k in range(1, NY):
+                gcopy(k).wait_recv()
+            gains.start()
+        mid.wait(t - 2)
+        for k in range(passed[max(t - 2, 0)], passed[t - 1]):
+            for flow in both(k):
+                over_y.wait(flow, k)
+                side_copy(flow, k).start()
+        if t >= 6:
+            drain(t - 6)
+            late.drain(t - 6)
+
+    for k in range(9):
+        for flow in both(k):
+            side_copy(flow, k).wait_recv()
+    gains.wait_recv()
+
+    def settle():
+        for k in range(5, 9):
+            drain(k)
+        for k in range(9):
+            for flow in both(k):
+                side_copy(flow, k).wait_send()
+        blocks.finish()
+        gains.wait_send()
+        for k in range(1, NY):
+            ycopy(k).wait_send()
+            gcopy(k).wait_send()
+
+    return settle
 
 
 def normalize(values):
@@ -405,7 +373,9 @@
 
 
 OWN = ROWS // 2
-CHUNK = 512
+SELF = 11
+FAR = 7
+CHUNK = 1024
 CHUNKS = WIDTH // CHUNK
 PIECES = 4
 PIECE = WIDTH // PIECES
@@ -489,8 +459,8 @@
 
         mean = tiled(row_mean(total))
         squares = jnp.zeros((OWN, 128), f32)
-        acc = jnp.zeros((OWN, HID), f32)
-        columns = jnp.zeros((8, 128), f32)
+        acc = jnp.zeros((OWN + 16, HID), f32)
+        ones = jnp.ones((16, CHUNK), bf16)
         for j in range(CHUNKS):
             cols = cols_of(j)
             centred = x[:, cols].astype(f32) - mean
@@ -498,9 +468,9 @@
             low = centred.astype(bf16)
             cb[s, :, cols] = low
             part = weight(s, j, 0)
-            acc = acc + jnp.dot(low, part, preferred_element_type=f32)
-            columns = columns + jnp.sum(part.astype(f32).reshape(CHUNK // 8, 8, HID), axis=0)
-        wsum[s] = columns
+            acc = acc + jnp.dot(jnp.concatenate([low, ones], axis=0), part, preferred_element_type=f32)
+        wsum[s] = acc[OWN : OWN + 8]
+        acc = acc[:OWN]
         spread = lax.rsqrt(row_mean(squares) + eps_norm)
         inv[s] = spread
         pre_act = acc * spread
@@ -557,7 +527,7 @@
         s = last - i
         scaled_pre, pre_act = inner(s, hidden_grad)
         pre_f = scaled_pre.astype(f32)
-        shift = tiled(row_mean(pre_f * jnp.sum(wsum[s], axis=0, keepdims=True)))
+        shift = tiled(row_mean(pre_f * wsum[s, 0:1]))
         slope = tiled(row_mean(pre_f * pre_act) * inv[s])
         gain = tiled(gain_of(s - 1))
         slot = lax.rem(s + 1, 2)
@@ -590,13 +560,19 @@
     send_pg().wait()
     for p in range(PIECES):
         send_out(p).wait()
+    def store(j, half, columns):
+        rows = columns.astype(bf16).T.reshape(CHUNK // 256, NX, SHARD, HID)
+        for i in range(CHUNK // 256):
+            slot = lax.rem(j * (CHUNK // 256) + i - me.z + SELF + NZ, NZ)
+            grad_ref[slot, :, :, pl.ds(half * HID, HID)] = rows[i]
+
     pg_a, pg_b, hid_a, hid_b = pg[me.c], pg_in[...], hid[mine], hid_in[...]
     for j in range(CHUNKS):
         cols = cols_of(j)
         first = contract_first(pg_a, cb[mine, :, cols]) + contract_first(pg_b, cb_in[:, cols])
-        grad_ref[span(j), :, :, :HID] = first.astype(bf16).T.reshape(CHUNK // 256, NX, SHARD, HID)
+        store(j, 0, first)
         second = contract_first(hid_a, out[me.c, :, cols]) + contract_first(hid_b, out_in[:, cols])
-        grad_ref[span(j), :, :, HID:] = second.astype(bf16).T.reshape(CHUNK // 256, NX, SHARD, HID)
+        store(j, 1, second)
 
 
 ROWS_Z, ROWS_X = 32, 32
@@ -609,18 +585,18 @@
         self.me, self.own, self.held, self.index = me, own, held, index
         self.zs, self.zr = sems
 
-    def target(self, flow, k):
-        return block_z(self.me, 1 - flow, k)
+    def slot(self, flow, k):
+        return (SELF + k if flow == 0 else SELF - k) % NZ
 
     def copy(self, flow, k):
         first = k % 2 == 1 or k == 8
         hop = 1 if k % 2 else 2
         to = self.me.at_z(hop if flow == 0 else -hop)
-        src = self.own(self.target(flow, k)) if first else self.held(flow, k + 2 if k < 6 or flow == 0 else 7)
+        src = self.own(self.slot(flow, k)) if first else self.held(flow, k + 2 if k < 6 or flow == 0 else 7)
         return remote(src, self.held(flow, k), self.zs.at[flow, k, self.index], self.zr.at[flow, k, self.index], to)
 
-    def begin(self):
-        for k in (8, 7, 5, 3, 1):
+    def begin(self, *distances):
+        for k in distances:
             for flow in range(2):
                 if k <= last_of(flow):
                     self.copy(flow, k).start()
@@ -631,7 +607,7 @@
             for i in ((7, 8) if k == 6 else (k + 1, k + 2)):
                 if i <= last_of(flow):
                     self.copy(flow, i).wait_recv()
-            own = self.own(self.target(flow, k))
+            own = self.own(self.slot(flow, k))
             total = own[...].astype(f32) + self.held(flow, into)[...].astype(f32)
             if into != k + 1:
                 total = total + self.held(flow, k + 1)[...].astype(f32)
@@ -644,7 +620,7 @@
                 self.copy(flow, k).wait_recv()
 
     def result(self):
-        total = self.own(self.me.z)[...].astype(f32)
+        total = self.own(SELF)[...].astype(f32)
         for flow in range(2):
             for k in (1, 2):
                 total = total + self.held(flow, k)[...].astype(f32)
@@ -657,18 +633,20 @@
 
 
 def finish(
-    me, grad_ref, master_ref, first_ref, second_ref, gain_ref, probe_ref,
+    me, settle, put, grad_ref, master_ref, first_ref, second_ref, gain_ref, probe_ref,
     out_ref, new_master_ref, new_first_ref, new_second_ref,
     fresh, ra, rb, xa, xa_out, xb, tb, share, near, far,
     zs, zr, xs, xr, ns, nr, ms, mr, *sems,
 ):
     def group_at(i):
-        ds, dx = i // NX, lax.rem(i, NX)
+        ds, dx = i // NX, i % NX
         return (lax.rem(me.s + ds, SECTIONS), me.z * NX + lax.rem(me.x + dx, NX))
 
-    def xbcopy(dx):
-        src = grad_ref.at[:, lax.rem(me.x + dx, NX), pl.ds(ROWS_Z, ROWS_X), :]
-        return remote(src, xb.at[dx], xs.at[1, dx], xr.at[1, dx], me.at_x(dx))
+    def xbcopy(dx, part):
+        span = slice(0, FAR) if part == 0 else slice(FAR, NZ)
+        src = grad_ref.at[span, lax.rem(me.x + dx, NX), pl.ds(ROWS_Z, ROWS_X), :]
+        sem = (1 + part, dx)
+        return remote(src, xb.at[dx, span], xs.at[sem], xr.at[sem], me.at_x(dx))
 
     def xacopy(dx):
         src = xa_out.at[lax.rem(me.x + dx, NX)]
@@ -686,35 +664,45 @@
 
     pieces = [piece_sum(0), piece_sum(1)]
     late = SumRoundZ(me, lambda z: tb.at[z], lambda flow, k: rb.at[flow, k], (zs, zr), 2)
+    def add(part):
+        for dx in range(1, NX):
+            xbcopy(dx, part).wait_recv()
+        for z in range(FAR) if part == 0 else range(FAR, NZ):
+            total = grad_ref[z, me.x, pl.ds(ROWS_Z, ROWS_X), :].astype(f32)
+            for dx in range(1, NX):
+                total = total + xb[dx, z].astype(f32)
+            tb[z] = total.astype(bf16)
+
     for piece in pieces:
-        piece.begin()
-    for dx in range(1, NX):
-        xbcopy(dx).start()
+        piece.begin(8, 7)
+    for part in range(2):
+        for dx in range(1, NX):
+            xbcopy(dx, part).start()
+        if part == 0:
+            for piece in pieces:
+                piece.begin(5)
+    settle()
     for piece in pieces:
         piece.step(6)
     for piece in pieces:
+        piece.begin(3)
+    add(0)
+    late.begin(8, 7, 5)
+    for piece in pieces:
         piece.step(4)
-    for dx in range(1, NX):
-        xbcopy(dx).wait_recv()
-
-    def add(z, carry):
-        total = grad_ref[z, me.x, pl.ds(ROWS_Z, ROWS_X), :].astype(f32)
-        for dx in range(1, NX):
-            total = total + xb[dx, z].astype(f32)
-        tb[z] = total.astype(bf16)
-        return carry
-
-    lax.fori_loop(0, NZ, add, 0)
-    late.begin()
+    for piece in pieces:
+        piece.begin(1)
+    late.step(6)
+    add(1)
+    late.begin(3, 1)
     for piece in pieces:
         piece.step(2)
-    late.step(6)
+    late.step(4)
     for i, piece in enumerate(pieces):
         piece.wait()
         xa_out[pl.ds(2 * i, 2)] = piece.result().astype(bf16)
     for dx in range(1, NX):
         xacopy(dx).start()
-    late.step(4)
     late.step(2)
     for dx in range(1, NX):
         xacopy(dx).wait_recv()
@@ -738,26 +726,28 @@
     def mcopy(k):
         return remote(far.at[0], far.at[k], ms.at[k], mr.at[k], me.at_z(k))
 
-    def n_start(i, carry):
+    def n_wait(i, carry):
+        ncopy(i).wait_recv()
+        return carry
+
+    def n_sent(i, carry):
+        ncopy(i).wait_send()
+        return carry
+
+    def m_sent(i, carry):
+        mcopy(i).wait_send()
+        return carry
+
+    def m_wait(i, carry):
+        mcopy(i).wait_recv()
+        return carry
+
+    for i in range(1, GROUP):
         ncopy(i).start()
-        return carry
-
-    def n_wait(i, carry):
-        ncopy(i).wait()
-        return carry
-
-    def m_start(i, carry):
-        mcopy(i).start()
-        return carry
-
-    def m_wait(i, carry):
-        mcopy(i).wait()
-        return carry
-
-    lax.fori_loop(1, GROUP, n_start, 0)
     lax.fori_loop(1, GROUP, n_wait, 0)
     far[0] = jnp.sum(near[...], axis=0)
-    lax.fori_loop(1, NZ, m_start, 0)
+    for k in (8, 7, 9, 6, 10, 5, 11, 4, 12, 3, 13, 2, 14, 1, 15):
+        mcopy(k).start()
     lax.fori_loop(1, NZ, m_wait, 0)
     norm_sq = jnp.sum(jnp.sum(far[...], axis=0), keepdims=True)
 
@@ -787,16 +777,28 @@
     blocks = BlocksRoundZ(me, early_part, early_block, sems[6:10], 2)
     blocks.begin()
     mid.begin()
+    for copy in put:
+        copy.start()
+    for piece in pieces:
+        piece.drain()
+    late.drain()
+    for dx in range(1, NX):
+        xbcopy(dx, 0).wait_send()
+        xbcopy(dx, 1).wait_send()
+        xacopy(dx).wait_send()
     blocks.launch()
-
-    def step(t, carry):
+    lax.fori_loop(1, GROUP, n_sent, 0)
+    lax.fori_loop(1, NZ, m_sent, 0)
+
+    for t in range(1, 7):
         mid.step(t)
         blocks.step(t)
         mid.pass_on(t - 1)
         mid.wait(t - 2)
-        return carry
-
-    lax.fori_loop(1, 7, step, 0)
+        if t >= 3:
+            mid.drain(t - 3)
+            blocks.drain(t - 3)
+
     values = probe_ref[...].astype(f32)
     normed = normalize(values)[0].astype(bf16)
     pre_act = jnp.zeros((TOK, HID), f32)
@@ -809,19 +811,9 @@
         part = fresh[z, :, :, HID:].reshape(256, HID)
         cols = slice(z * 256, (z + 1) * 256)
         out_ref[:, cols] = (values[:, cols] + gain * contract_last(hidden, part)).astype(bf16)
-    def drain(t, carry):
-        mid.drain(t)
-        blocks.drain(t)
-        return carry
-
-    lax.fori_loop(0, 5, drain, 0)
+    mid.drain(4)
+    blocks.drain(4)
     blocks.finish()
-    for piece in pieces:
-        piece.drain()
-    late.drain()
-    for dx in range(1, NX):
-        xbcopy(dx).wait_send()
-        xacopy(dx).wait_send()
 
 
 def partners(me):
@@ -830,57 +822,110 @@
     return ys + xs + [me.at_z(k) for k in (1, 2, -1, -2)] + [me.sibling()]
 
 
-N_GATHER, N_RELAY, N_FINISH = 27, 4, 18
+N_GATHER, N_RELAY = 26, 4
 
 
 def step_kernel(
-    w_ref, gain_ref, x_hbm, marks_ref, master_ref, first_ref, second_ref,
-    out_ref, new_master_ref, new_first_ref, new_second_ref,
-    w, gains, grad, probe,
+    w_ref, depth_hbm, counts_hbm, plan_hbm, x_hbm, master_hbm, first_hbm, second_hbm,
+    out_ref, new_master_hbm, new_first_hbm, new_second_hbm,
+    w, gains, grad, probe, gain_ref, marks_ref, master_ref, first_ref, second_ref,
+    depth_ref, counts_ref, plan_ref, new_master_ref, new_first_ref, new_second_ref,
     x, g, cb, inv, pre, hid, wsum, out, pg, cb_in, hid_in, out_in, pg_in, pr, pr_in,
     fresh, ra, rb, xa, xa_out, xb, tb, share, near, far,
     x_sem, *sems,
 ):
     me = Place()
     get_x = pltpu.make_async_copy(
-        x_hbm.at[pl.ds(pl.multiple_of(me.c * OWN, OWN), OWN)], x, x_sem
+        x_hbm.at[pl.ds(pl.multiple_of(me.c * OWN, OWN), OWN)], x, x_sem.at[0]
     )
+    state = [
+        pltpu.make_async_copy(src, dst, x_sem.at[i + 1])
+        for i, (src, dst) in enumerate(
+            (
+                (depth_hbm, depth_ref),
+                (counts_hbm, counts_ref),
+                (plan_hbm, plan_ref),
+                (master_hbm, master_ref),
+                (first_hbm, first_ref),
+                (second_hbm, second_ref),
+            )
+        )
+    ]
+    keep = pltpu.make_async_copy(w_ref, w.at[me.c, me.y, me.z, me.x], x_sem.at[7])
+    keep.start()
+    for get in state[:3]:
+        get.start()
     get_x.start()
+    for get in state[3:]:
+        get.start()
     greet(partners(me))
-    gather_all(me, w_ref, gain_ref, w, gains, *sems[:N_GATHER])
+
+    def ready():
+        for get in state[:3]:
+            get.wait()
+        gain_ref[...] = jnp.broadcast_to(lax.rsqrt(1.0 + depth_ref[...].astype(f32) / 8.0), (8, 128))
+        place_in_block = lax.broadcasted_iota(jnp.int32, (TOK, 128), 0)
+        for m in range(ROWS // TOK):
+            rows = pl.ds(m * TOK, TOK)
+            marks_ref[0, rows, :] = (place_in_block < counts_ref[0:1, m : m + 1]).astype(f32)
+            planned = jnp.broadcast_to((plan_ref[0:1, 15:16] == m).astype(f32), (TOK, 128))
+            marks_ref[1, rows, :] = planned
+
+    settle = gather_all(me, w_ref, keep, ready, w, gains, gain_ref, *sems[:N_GATHER])
     get_x.wait()
+    for get in state[3:]:
+        get.wait()
     relay(
         me, w, gains, marks_ref, grad, probe,
         x, g, cb, inv, pre, hid, wsum, out, pg, cb_in, hid_in, out_in, pg_in, pr, pr_in,
         *sems[N_GATHER : N_GATHER + N_RELAY],
     )
+    put = [
+        pltpu.make_async_copy(src, dst, x_sem.at[i])
+        for i, (src, dst) in enumerate(
+            (
+                (new_master_ref, new_master_hbm),
+                (new_first_ref, new_first_hbm),
+                (new_second_ref, new_second_hbm),
+            )
+        )
+    ]
     finish(
-        me, grad, master_ref, first_ref, second_ref, gain_ref, probe,
+        me, settle, put, grad, master_ref, first_ref, second_ref, gain_ref, probe,
         out_ref, new_master_ref, new_first_ref, new_second_ref,
         fresh, ra, rb, xa, xa_out, xb, tb, share, near, far,
         *sems[N_GATHER + N_RELAY :],
     )
+    for copy in put:
+        copy.wait()
+
+
+def hand_out_kernel(*refs):
+    for i in range(4):
+        refs[4 + i][...] = refs[i][...]
 
 
 def shards(inputs, stashed, master, first_moment, second_moment, counts, plan, layer_index):
-    gain_tile = jnp.full((8, 128), lax.rsqrt(1.0 + layer_index.astype(f32) / 8.0)[0], f32)
-    row_pos = lax.broadcasted_iota(jnp.int32, (16, TOK), 1)
-    valid = row_pos < counts[0][:, None]
-    chosen = lax.broadcasted_iota(jnp.int32, (16, TOK), 0) == plan[15]
-    marks = jnp.stack([valid, chosen]).astype(f32).reshape(2, ROWS, 1)
     state = jax.ShapeDtypeStruct((SHARD, 2 * HID), f32)
     vmem = pl.BlockSpec(memory_space=pltpu.VMEM)
+    anywhere = pl.BlockSpec(memory_space=pl.ANY)
     chunks = (NZ, NX, SHARD, 2 * HID)
     probe_out, new_master, new_first, new_second = pl.pallas_call(
         step_kernel,
         out_shape=(jax.ShapeDtypeStruct((TOK, WIDTH), bf16), state, state, state),
-        in_specs=[vmem, vmem, pl.BlockSpec(memory_space=pl.ANY), vmem, vmem, vmem, vmem],
-        out_specs=(vmem,) * 4,
+        in_specs=[anywhere] * 8,
+        out_specs=(vmem, anywhere, anywhere, anywhere),
         scratch_shapes=[
             pltpu.VMEM((2, NY, *chunks), bf16),
             pltpu.VMEM((2, NY, 8, 128), f32),
             pltpu.VMEM(chunks, bf16),
             pltpu.VMEM((TOK, WIDTH), bf16),
+            pltpu.VMEM((8, 128), f32),
+            pltpu.VMEM((2, ROWS, 128), f32),
+            *[pltpu.VMEM((SHARD, 2 * HID), f32)] * 3,
+            pltpu.VMEM((1, 1), jnp.int32),
+            *[pltpu.VMEM((1, ROWS // TOK), jnp.int32)] * 2,
+            *[pltpu.VMEM((SHARD, 2 * HID), f32)] * 3,
             pltpu.VMEM((OWN, WIDTH), bf16),
             pltpu.VMEM((OWN, WIDTH), bf16),
             pltpu.VMEM((SECTIONS, OWN, WIDTH), bf16),
@@ -906,10 +951,9 @@
             pltpu.VMEM((SHARD, 2 * HID), f32),
             pltpu.VMEM((GROUP, 8, 128), f32),
             pltpu.VMEM((NZ, 8, 128), f32),
-            DMA,
+            DMA((8,)),
             *[DMA((NY,))] * 4,
             *[DMA((3, 9))] * 2,
-            DMA((2,)),
             *ROUND_SEMS,
             *ROUND_SEMS,
             *BLOCK_SEMS,
@@ -917,7 +961,7 @@
             *[DMA((3,))] * 2,
             *[DMA((PIECES + 1,))] * 2,
             *[DMA((2, 9, 3))] * 2,
-            *[DMA((2, NX))] * 2,
+            *[DMA((3, NX))] * 2,
             *[DMA((GROUP,))] * 2,
             *[DMA((NZ,))] * 2,
             *ROUND_SEMS,
@@ -928,10 +972,18 @@
         ),
         name="optimizer_step",
     )(
-        stashed[0], gain_tile, inputs.reshape(ROWS, WIDTH),
-        jnp.broadcast_to(marks, (2, ROWS, 128)), master[0], first_moment[0], second_moment[0],
+        stashed[0], layer_index.reshape(1, 1), counts, plan.reshape(1, 16),
+        inputs.reshape(ROWS, WIDTH), master[0], first_moment[0], second_moment[0],
     )
-    return (probe_out[None], new_master[None], new_first[None], new_second[None])
+    results = (probe_out[None], new_master[None], new_first[None], new_second[None])
+    return pl.pallas_call(
+        hand_out_kernel,
+        out_shape=tuple(jax.ShapeDtypeStruct(r.shape, r.dtype) for r in results),
+        in_specs=[vmem] * 4,
+        out_specs=(vmem,) * 4,
+        compiler_params=pltpu.CompilerParams(vmem_limit_bytes=60 * 2**20),
+        name="hand_out",
+    )(*results)
 
 
 def solution(mesh):

time: 189 us -> 176 us (0.931)
  local copies, waits for them, and re-layouts: 9.71 us -> 0 us
  Pallas kernels: 176 us -> 174 us
    unnamed x4 -> x0, local copies, waits for them, and re-layouts: 5.98 us -> none
    pallas_call x1, Pallas kernels: 176 us -> 173 us  [shards(): pl.pallas_call(step_kernel, out_shape=(jax.ShapeDtypeStruct((TOK, WIDTH),...]
where the time goes in v4:
time: 176 us
  Pallas kernels  174 us (99%)
    pallas_call x1, Pallas kernels, shards(): pl.pallas_call(step_kernel, out_shape=(jax.ShapeDtypeStruct((TOK, WIDTH),...  173 us

profile of v4, /device:TPU:24, one launch (start us, length us, event | category | flops | bytes accessed | tf_op | source)
XLA Modules:
  0.0 175.6 jit_solution(6218623288219381879)
XLA Ops:
  1.3 172.7 %optimizer_step.1 = (bf16[16,4096]{1,0:T(8,128)(2,1)}, f32[64,256]{1,0:T(8,128)}, f32[64,256]{1,0:T(8,128)}, f32[64,256]{1,0:T(8,128)}) custom-call(bf16[64,256]{1,0:T(8,128)(2,1)} %bitcast.20, s32[1,1]{1,0:T(1,128)} %bitcast.11.depth_hbm, s32[1,16]{1,0:T(1,128)} %counts_hbm.1, s32[1,16]{1,0:T(1,128)} %bitcast.21, bf16[256,4096]{1,0:T(8,128)(2,1)} %bitcast.12, ...), custom_call_target="tpu_custom_call" | custom-call | tf_op jit(solution)/shard_map/optimizer_step/pallas_call | solution.py:913
  173.9 1.7 hand_out.1

commit v5 on v4

--- a/solution.py
+++ b/solution.py
@@ -266,7 +266,7 @@
     def early_block(z, piece):
         return all_ref.at[me.c, pl.ds(2 * piece, 2), z, :, pl.ds(0, ROWS_XZ)]
 
-    late = RoundZ(me, late_part, sems[0:6], 2)
+    late = RoundZ(me, late_part, sems[0:6], 1)
     mid = RoundZ(me, mid_part, sems[6:12], 1)
     blocks = BlocksRoundZ(me, early_part, early_block, sems[12:16], 1)
     over_y = OverX(me, late_column, me.at_y, me.y, sems[16:20])
@@ -295,30 +295,26 @@
         for flow in both(k):
             over_y.drain(flow, k)
 
-    passed = [max(0, min(9, (t - 2) * 9 // 7)) for t in range(12)]
-    for t in range(1, 11):
+    for t in range(1, 13):
         late.step(t)
-        mid.step(t)
+        mid.step(t - 1)
         late.pass_on(t - 1)
-        mid.pass_on(t - 1)
+        mid.pass_on(t - 2)
         late.wait(t - 2)
-        for k in late.steps_of(t - 2):
-            for flow in both(k):
-                over_y.send(flow, k)
-        for k in range(passed[t - 1], passed[t]):
-            over_y.pass_on(k)
-        blocks.step(t - 1)
-        if t == 1:
+        for flow in both(t - 2):
+            over_y.send(flow, t - 2)
+        mid.wait(t - 3)
+        over_y.pass_on(t - 3)
+        if t == 2:
             blocks.launch()
+        blocks.step(t - 2)
         if t == 4:
             for k in range(1, NY):
                 gcopy(k).wait_recv()
             gains.start()
-        mid.wait(t - 2)
-        for k in range(passed[max(t - 2, 0)], passed[t - 1]):
-            for flow in both(k):
-                over_y.wait(flow, k)
-                side_copy(flow, k).start()
+        for flow in both(t - 4):
+            over_y.wait(flow, t - 4)
+            side_copy(flow, t - 4).start()
         if t >= 6:
             drain(t - 6)
             late.drain(t - 6)
@@ -329,8 +325,9 @@
     gains.wait_recv()
 
     def settle():
-        for k in range(5, 9):
+        for k in range(7, 9):
             drain(k)
+            late.drain(k)
         for k in range(9):
             for flow in both(k):
                 side_copy(flow, k).wait_send()

time: 176 us -> 170 us (0.966)
  Pallas kernels: 174 us -> 169 us
    pallas_call x1, Pallas kernels: 173 us -> 167 us  [shards(): pl.pallas_call(step_kernel, out_shape=(jax.ShapeDtypeStruct((TOK, WIDTH),...]
where the time goes in v5:
time: 170 us
  Pallas kernels  169 us (99%)
    pallas_call x1, Pallas kernels, shards(): pl.pallas_call(step_kernel, out_shape=(jax.ShapeDtypeStruct((TOK, WIDTH),...  167 us

profile of v5, /device:TPU:24, one launch (start us, length us, event | category | flops | bytes accessed | tf_op | source)
XLA Modules:
  0.0 170.3 jit_solution(14058913701993815106)
XLA Ops:
  1.3 167.3 %optimizer_step.1 = (bf16[16,4096]{1,0:T(8,128)(2,1)}, f32[64,256]{1,0:T(8,128)}, f32[64,256]{1,0:T(8,128)}, f32[64,256]{1,0:T(8,128)}) custom-call(bf16[64,256]{1,0:T(8,128)(2,1)} %bitcast.20, s32[1,1]{1,0:T(1,128)} %bitcast.11.depth_hbm, s32[1,16]{1,0:T(1,128)} %counts_hbm.1, s32[1,16]{1,0:T(1,128)} %bitcast.21, bf16[256,4096]{1,0:T(8,128)(2,1)} %bitcast.12, ...), custom_call_target="tpu_custom_call" | custom-call | tf_op jit(solution)/shard_map/optimizer_step/pallas_call | solution.py:910
  168.6 1.7 hand_out.1

commit v6 on v5

--- a/solution.py
+++ b/solution.py
@@ -745,6 +745,7 @@
     far[0] = jnp.sum(near[...], axis=0)
     for k in (8, 7, 9, 6, 10, 5, 11, 4, 12, 3, 13, 2, 14, 1, 15):
         mcopy(k).start()
+    normed = normalize(probe_ref[...].astype(f32))[0].astype(bf16)
     lax.fori_loop(1, NZ, m_wait, 0)
     norm_sq = jnp.sum(jnp.sum(far[...], axis=0), keepdims=True)
 
@@ -797,7 +798,6 @@
             blocks.drain(t - 3)
 
     values = probe_ref[...].astype(f32)
-    normed = normalize(values)[0].astype(bf16)
     pre_act = jnp.zeros((TOK, HID), f32)
     for z in range(NZ):
         part = fresh[z, :, :, :HID].reshape(256, HID)

time: 170 us -> 170 us (level)
  no operation moved by 1% of the time
where the time goes in v6:
time: 170 us
  Pallas kernels  169 us (99%)
    pallas_call x1, Pallas kernels, shards(): pl.pallas_call(step_kernel, out_shape=(jax.ShapeDtypeStruct((TOK, WIDTH),...  167 us

profile of v6, /device:TPU:24, one launch (start us, length us, event | category | flops | bytes accessed | tf_op | source)
XLA Modules:
  0.0 170.1 jit_solution(8309433753715549213)
XLA Ops:
  1.3 167.1 %optimizer_step.1 = (bf16[16,4096]{1,0:T(8,128)(2,1)}, f32[64,256]{1,0:T(8,128)}, f32[64,256]{1,0:T(8,128)}, f32[64,256]{1,0:T(8,128)}) custom-call(bf16[64,256]{1,0:T(8,128)(2,1)} %bitcast.20, s32[1,1]{1,0:T(1,128)} %bitcast.11.depth_hbm, s32[1,16]{1,0:T(1,128)} %counts_hbm.1, s32[1,16]{1,0:T(1,128)} %bitcast.21, bf16[256,4096]{1,0:T(8,128)(2,1)} %bitcast.12, ...), custom_call_target="tpu_custom_call" | custom-call | tf_op jit(solution)/shard_map/optimizer_step/pallas_call | solution.py:910
  168.4 1.7 hand_out.1
